TPU v7x, 32 devices: a whole 2x2x4 slice. The times are simulated.
32 devices in a mesh: view: 4 (over y, x), sent: 4 (over z), col: 2 (over core).
Axes of the slice: x: 2, y: 2, z: 4, core: 2. Of those that a mesh axis runs over, the one named last changes fastest.
Arguments:
- sketched: bfloat16 [12, 4096, 2048], P('view', 'sent', 'col')
- widths: int32 [12], P('view'), may hold values from 256 to 2048, as said below
- inv_factor: float32 [12, 2048, 2048], P('view', 'sent', 'col'), as said below
- shared: bfloat16 [4096, 256], P('sent'), may hold values from -6 to 6
Outputs:
- loadings: float32 [12, 2048, 256], P('view', 'col')
- updated: float32 [4096, 256], P('sent')
Inputs may be any that keep to these rules, and one draw needn't show every extreme that they name: `widths`: every width is a multiple of 128; in every draw one view has width 2048 and another 2 * 128. Each inv_factor[j] is lower triangular with diagonal entries of 1 to 2.
All inputs are finite; a program needn't handle non-finite values.
Results may differ from a plain program's by a relative error of at most 0.0026.
Values sent between devices are 32-bit elements; how exact they have to be, the bound alone decides.
No kernel may reach another device: no remote copies, remote signals or barrier semaphores. Data moves between devices by JAX's collectives and lax.ppermute only.
A program may use at most 128 MiB of HBM per device.

v0:
```python
import functools
import math

import jax
import jax.numpy as jnp
from jax import lax
from jax.experimental import pallas as pl
from jax.experimental.pallas import tpu as pltpu
from jax.sharding import PartitionSpec as P

CHUNK = 256
LANES = 2
PANEL = 32


class Line:
    def __init__(self, lanes, sent_index, col_index):
        self.lanes, self.sent_index, self.col_index = lanes, sent_index, col_index
        self.inner = (sent_index == 1) | (sent_index == 2)
        self.slot, self.chunks, self.pairs, self.totals, self.finals = 0, {}, {}, {}, {}
        self.arrived = {}

    def pairs_of(self, k, stage):
        if k not in self.chunks:
            return []
        _, first, spread = self.chunks[k]
        always = lambda f: True
        if spread:
            hops = (
                {(0, 1): always, (3, 2): lambda f: f < 3},
                {(1, 2): always, (2, 1): lambda f: f <= 1},
                {(2, 3): always, (1, 0): lambda f: f <= 0},
            )
        else:
            hops = (
                {(3, 2): always, (0, 1): lambda f: f <= 0},
                {(2, 1): always, (1, 2): lambda f: f <= 1},
                {(1, 0): always, (2, 3): lambda f: f <= 2},
            )
        cores = len(first)
        return [
            (a * cores + c, b * cores + c)
            for c in range(cores)
            for (a, b), wanted in hops[stage].items()
            if wanted(first[c])
        ]

    def step(self, term=None, first=None, spread=None):
        k = self.slot
        self.slot += 1
        self.collect(k - self.lanes)
        middle, last = k - self.lanes, k - 2 * self.lanes
        if term is not None:
            self.chunks[k] = (term, first, spread)
        ends, pair = term, self.pairs.get(middle)
        if last in self.totals:
            total = self.totals[last]
            ends = total if term is None else jnp.where(self.inner, total, term)
        if ends is not None and pair is not None:
            ends, pair = lax.optimization_barrier((ends, pair))
        axes, ends_in, pair_in = ("sent", "col"), None, None
        if ends is not None:
            perm = self.pairs_of(k, 0) + self.pairs_of(last, 2)
            ends_in = lax.ppermute(ends, axes, perm)
        if pair is not None:
            pair_in = lax.ppermute(pair, axes, self.pairs_of(middle, 1))
        self.arrived[k] = (ends, ends_in, pair_in)

    def collect(self, k):
        if k not in self.arrived:
            return
        ends, ends_in, pair_in = self.arrived.pop(k)
        middle, last = k - self.lanes, k - 2 * self.lanes
        following = self.arrived.get(k + 1, (None,))[0] if self.lanes > 1 else None
        tied = [v for v in (following, ends_in, pair_in) if v is not None]
        tied = list(lax.optimization_barrier(tuple(tied)))
        if following is not None:
            del tied[0]
        if ends_in is not None:
            ends_in = tied.pop(0)
        if pair_in is not None:
            self.totals[middle] = self.pairs[middle] + tied.pop(0)
        if k in self.chunks:
            self.pairs[k] = self.chunks[k][0] + ends_in
        if last in self.totals:
            old, first, _ = self.chunks[last]
            alone = (self.sent_index == 3) & (self.col_index >= [f == 3 for f in first].index(True)) \
                if 3 in first else None
            outer = ends_in if alone is None else jnp.where(alone, ends_in + old, ends_in)
            self.finals[last] = jnp.where(self.inner, ends, outer)


def pieces(x):
    high = x.astype(jnp.bfloat16)
    rest = x - high.astype(jnp.float32)
    middle = rest.astype(jnp.bfloat16)
    return high, middle, (rest - middle.astype(jnp.float32)).astype(jnp.bfloat16)


def whiten_kernel(scale, gram_ref, merged_ref, out_ref, work):
    size = gram_ref.shape[0]
    tile = (8, 128)
    work[:, :size] = gram_ref[...]
    rows = lax.broadcasted_iota(jnp.int32, (size, size), 0)
    work[:, size:] = (rows == lax.broadcasted_iota(jnp.int32, (size, size), 1)).astype(jnp.float32)
    sublane = lax.broadcasted_iota(jnp.int32, tile, 0)
    for panel in range(0, size, PANEL):
        end = panel + PANEL
        start = panel // 128 * 128
        stop = size + start + 128
        for block in range(panel, end, 8):
            lanes = range(start, stop, 128)
            cols = [
                [
                    jnp.broadcast_to(
                        work[t : t + 8, start : start + 128][:, block - start + k][:, None], tile
                    )
                    for k in range(8)
                ]
                for t in range(block, end, 8)
            ]
            low = [
                [jnp.broadcast_to(cols[0][k][i : i + 1], tile) for k in range(i + 1)]
                for i in range(8)
            ]
            inverse = []
            for k in range(8):
                pivot = low[k][k]
                root = lax.rsqrt(pivot)
                root = root * (1.5 - 0.5 * pivot * root * root)
                inverse.append(root)
                for i in range(k + 1, 8):
                    low[i][k] = low[i][k] * root
                for i in range(k + 1, 8):
                    for m in range(k + 1, i + 1):
                        low[i][m] = low[i][m] - low[i][k] * low[m][k]
            for t in range(1, len(cols)):
                for k in range(8):
                    value = cols[t][k]
                    for m in range(k):
                        value = value - low[k][m] * cols[t][m]
                    cols[t][k] = value * inverse[k]
            for lane in lanes:
                here = slice(lane, lane + 128)
                old = work[block : block + 8, here]
                done, new = [], old
                for k in range(8):
                    value = jnp.broadcast_to(old[k : k + 1], tile)
                    for m in range(k):
                        value = value - low[k][m] * done[m]
                    done.append(value * inverse[k])
                    new = jnp.where(sublane == k, done[k], new)
                work[block : block + 8, here] = new
                for t in range(1, len(cols)):
                    at = slice(block + 8 * t, block + 8 * t + 8)
                    value = work[at, here]
                    for k in range(8):
                        value = value - cols[t][k] * done[k]
                    work[at, here] = value
        if end < size:
            first = end // 128 * 128
            upper = pieces(work[panel:end, first:size])
            right = pieces(work[panel:end, first:stop])
            a = jnp.concatenate([upper[i] for i in (0, 0, 1, 1, 0, 2)])
            b = jnp.concatenate([right[i] for i in (0, 1, 0, 1, 2, 0)])
            update = lax.dot_general(
                a, b, (((0,), (0,)), ((), ())), preferred_element_type=jnp.float32
            )
            work[end:, first:stop] -= update[end - first :]
    a = pieces(merged_ref[...])
    b = pieces(work[:, size:] * scale)
    total = 0.0
    for i, j in ((1, 1), (0, 2), (2, 0), (0, 1), (1, 0), (0, 0)):
        total += lax.dot_general(
            a[i], b[j], (((1,), (1,)), ((), ())), preferred_element_type=jnp.float32
        )
    out_ref[...] = total


def whiten(gram, merged, scale):
    size = gram.shape[0]
    return pl.pallas_call(
        functools.partial(whiten_kernel, scale),
        out_shape=jax.ShapeDtypeStruct(merged.shape, jnp.float32),
        in_specs=[pl.BlockSpec(memory_space=pltpu.VMEM)] * 2,
        out_specs=pl.BlockSpec(memory_space=pltpu.VMEM),
        scratch_shapes=[pltpu.VMEM((size, 2 * size), jnp.float32)],
        compiler_params=pltpu.CompilerParams(vmem_limit_bytes=32 * 2**20),
        name="whiten",
    )(gram, merged)


def shards(sketched, widths, inv_factor, shared):
    view_count, row_count, col_half = sketched.shape
    factor_rows = inv_factor.shape[1]
    sent_size = lax.axis_size("sent")
    view_size = lax.axis_size("view")
    core_count = lax.axis_size("col")
    total_rows = row_count * sent_size
    scale = 1.0 / math.sqrt(total_rows)
    high = lax.Precision.HIGH
    highest = lax.Precision.HIGHEST
    col_index = lax.axis_index("col")
    sent_index = lax.axis_index("sent")
    col_pos = col_index * col_half + jnp.arange(col_half)
    keep_cols = (col_pos[None, :] < widths[:, None]).astype(jnp.float32)[:, :, None]
    row_pos = sent_index * factor_rows + jnp.arange(factor_rows)
    keep_rows = (row_pos[None, :] < widths[:, None]).astype(jnp.float32)[:, :, None]
    use_line = sent_size == 4 and core_count == 2 and col_half % (2 * CHUNK) == 0

    chunk = CHUNK if use_line else col_half
    per_view = col_half // chunk
    order = [q + h for q in range(per_view // 2) for h in (0, per_view // 2)] or [0]
    back_order = sorted(range(per_view), key=order.__getitem__)
    slots = [(j, q) for j in range(view_count) for q in order]
    firsts = [
        [(c * col_half + q * chunk) // factor_rows for c in range(core_count)] for _, q in slots
    ]

    def keep_of(j, q):
        return keep_cols[j, q * chunk : (q + 1) * chunk]

    down = (((0,), (0,)), ((), ()))
    def first_half(proj, j):
        proj = jnp.concatenate([proj[at] for at in back_order])
        half_part = jnp.dot(inv_factor[j], proj, precision=high)
        if use_line:
            perm = [
                (s * 2 + c, s * 2 + 1 - c)
                for s in range(sent_size)
                for c in range(2)
                if (s + 1) * factor_rows > col_half
            ]
            half = half_part + lax.ppermute(half_part, ("sent", "col"), perm)
        else:
            half = lax.psum(half_part, "col")
        return half * keep_rows[j]

    def cut(whole):
        return [whole[q * chunk : (q + 1) * chunk] for q in order]

    def term_of(features):
        return scale * lax.dot_general(features, shared, down, preferred_element_type=jnp.float32)

    terms = []
    for j in range(view_count):
        terms += cut(term_of(sketched[j]))

    def back_terms(proj, j):
        return cut(
            lax.dot_general(
                inv_factor[j], first_half(proj, j), down, precision=high,
                preferred_element_type=jnp.float32,
            )
        )

    if use_line:
        line = Line(LANES, sent_index, col_index)
        for term, first in zip(terms, firsts):
            line.step(term, first, True)
        done = 0
        while done < len(slots):
            while done + per_view - 1 not in line.finals:
                line.step()
            proj = [line.finals[done + q] * keep_of(*slots[done + q]) for q in range(per_view)]
            for q, term in enumerate(back_terms(proj, slots[done][0])):
                line.step(term, firsts[q], False)
            done += per_view
        begin = line.slot - len(slots)
        for _ in range(3 * LANES):
            line.step()
        sums = [line.finals[begin + k] for k in range(len(slots))]
    else:
        sums = []
        for j in range(view_count):
            proj = [lax.psum(terms[j], "sent") * keep_of(j, 0)]
            sums += [lax.psum(t, "sent") for t in back_terms(proj, j)]
    loads = [total * keep_of(*slot) for total, slot in zip(sums, slots)]
    loads = [loads[j * per_view + at] for j in range(view_count) for at in back_order]
    loadings = jnp.concatenate(loads).reshape(view_count, col_half, -1)
    contrib = 0.0
    for j in range(view_count):
        whole = jnp.concatenate(loads[j * per_view : (j + 1) * per_view]).astype(jnp.bfloat16)
        contrib += jnp.dot(sketched[j], whole, preferred_element_type=jnp.float32)

    if view_size == 4 and core_count == 2:
        part_rows = row_count // 2
        near = lambda bit: [(v, v ^ bit) for v in range(view_size)]
        swap = [(0, 1), (1, 0)]
        mine = lax.dynamic_slice_in_dim(contrib, col_index * part_rows, part_rows)
        other = lax.dynamic_slice_in_dim(contrib, (1 - col_index) * part_rows, part_rows)
        mine = mine + lax.ppermute(other, "col", swap)
        upper, lower_part = mine[: part_rows // 2], mine[part_rows // 2 :]
        upper = upper + lax.ppermute(upper, "view", near(1))
        lower_part = lower_part + lax.ppermute(lower_part, "view", near(2))
        upper = upper + lax.ppermute(upper, "view", near(2))
        lower_part = lower_part + lax.ppermute(lower_part, "view", near(1))
        mine = jnp.concatenate([upper, lower_part])
        other = lax.ppermute(mine, "col", swap)
        merged = jnp.concatenate(
            [jnp.where(col_index == 0, mine, other), jnp.where(col_index == 0, other, mine)]
        )
        width = mine.shape[1] // 2
        gram = lax.dot_general(mine, mine, (((0,), (0,)), ((), ())), precision=highest)
        left, right = gram[:, :width], gram[:, width:]
        gram = jnp.where(col_index == 0, left, right)
        gram = gram + lax.ppermute(jnp.where(col_index == 0, right, left), "col", swap)
    else:
        merged = lax.psum(contrib, ("view", "col"))
        gram = lax.dot_general(merged, merged, (((0,), (0,)), ((), ())), precision=highest)
        width = gram.shape[1] // core_count
        gram = lax.dynamic_slice_in_dim(gram, col_index * width, width, axis=1)

    if sent_size & (sent_size - 1) == 0:
        bit = 1
        while bit < sent_size:
            gram = gram + lax.ppermute(gram, "sent", [(s, s ^ bit) for s in range(sent_size)])
            bit *= 2
    else:
        gram = lax.psum(gram, "sent")
    if core_count == 2:
        other = lax.ppermute(gram, "col", [(0, 1), (1, 0)])
        gram = jnp.concatenate(
            [jnp.where(col_index == 0, gram, other), jnp.where(col_index == 0, other, gram)],
            axis=1,
        )
    else:
        gram = lax.all_gather(gram, "col", axis=1, tiled=True)
    updated = whiten(gram, merged, math.sqrt(total_rows))
    return (loadings, updated)


def solution(mesh):
    return jax.shard_map(
        shards,
        mesh=mesh,
        in_specs=(P("view", "sent", "col"), P("view"), P("view", "sent", "col"), P("sent", None)),
        out_specs=(P("view", "col", None), P("sent", None)),
        check_vma=False,
    )
```

profile of v0, /device:TPU:0, one launch (start us, length us, event | category | flops | bytes accessed | tf_op | source)
XLA Modules:
  0.0 252.3 jit_solution(12019210651841281169)
XLA Ops:
  1.7 2.8 %fusion.45 = f32[1024,256]{1,0:T(8,128)S(1)} fusion(bf16[1024,256]{1,0:T(8,128)(2,1)S(1)} %copy-done, bf16[3,1024,1024]{2,1,0:T(8,128)(2,1)} %param.4), kind=kOutput, calls=%fused_computation.39 | convolution fusion | flops 537133056 | bytes 3670016 | tf_op jit(solution)/shard_map/dot_general | solution.py:243
  5.2 4.9 %collective-permute-start = (f32[256,256]{1,0:T(8,128)}, f32[256,256]{1,0:T(8,128)S(1)}, u32[]{:S(2)}, u32[]{:S(2)}) collective-permute-start(f32[256,256]{1,0:T(8,128)} %get-tuple-element.250), channel_id=1, source_target_pairs={{0,2},{6,4},{1,3},{7,5},{8,10},{14,12},{9,11},{15,13},{16,18},{22,... | collective-permute-start | bytes 786440 | tf_op jit(solution)/shard_map/ppermute | solution.py:64
  11.5 1.7 fusion.54
  13.2 2.3 fusion.57
  17.2 4.3 %collective-permute-start.2 = (f32[256,256]{1,0:T(8,128)S(1)}, f32[256,256]{1,0:T(8,128)S(1)}, u32[]{:S(2)}, u32[]{:S(2)}) collective-permute-start(f32[256,256]{1,0:T(8,128)S(1)} %get-tuple-element.102), channel_id=1, source_target_pairs={{0,2},{6,4},{1,3},{7,5},{8,10},{14,12},{9,11},{15,13},{16,18},{22,... | collective-permute-start | bytes 786440 | tf_op jit(solution)/shard_map/ppermute | solution.py:64
  21.5 1.4 collective-permute-start.3
  23.1 4.2 %collective-permute-start.4 = (f32[256,256]{1,0:T(8,128)S(1)}, f32[256,256]{1,0:T(8,128)S(1)}, u32[]{:S(2)}, u32[]{:S(2)}) collective-permute-start(f32[256,256]{1,0:T(8,128)S(1)} %get-tuple-element.104), channel_id=1, source_target_pairs={{0,2},{6,4},{1,3},{8,10},{14,12},{9,11},{16,18},{22,20},{17,19},{2... | collective-permute-start | bytes 786440 | tf_op jit(solution)/shard_map/ppermute | solution.py:64
  29.5 4.5 %collective-permute-start.6 = (f32[256,256]{1,0:T(8,128)S(1)}, f32[256,256]{1,0:T(8,128)S(1)}, u32[]{:S(2)}, u32[]{:S(2)}) collective-permute-start(f32[256,256]{1,0:T(8,128)S(1)} %get-tuple-element.108), channel_id=1, source_target_pairs={{0,2},{6,4},{1,3},{7,5},{4,6},{2,0},{5,7},{8,10},{14,12},{9,11},{1... | collective-permute-start | bytes 786440 | tf_op jit(solution)/shard_map/ppermute | solution.py:64
  35.8 5.0 %collective-permute-start.8 = (f32[256,256]{1,0:T(8,128)S(1)}, f32[256,256]{1,0:T(8,128)S(1)}, u32[]{:S(2)}, u32[]{:S(2)}) collective-permute-start(f32[256,256]{1,0:T(8,128)S(1)} %add_select_fusion.30), channel_id=1, source_target_pairs={{0,2},{6,4},{1,3},{4,6},{5,7},{8,10},{14,12},{9,11},{12,14},{13,15... | collective-permute-start | bytes 786440 | tf_op jit(solution)/shard_map/ppermute | solution.py:64
  42.7 5.1 %collective-permute-start.10 = (f32[256,256]{1,0:T(8,128)S(1)}, f32[256,256]{1,0:T(8,128)S(1)}, u32[]{:S(2)}, u32[]{:S(2)}) collective-permute-start(f32[256,256]{1,0:T(8,128)S(1)} %get-tuple-element.116), channel_id=1, source_target_pairs={{0,2},{6,4},{1,3},{7,5},{4,6},{2,0},{5,7},{8,10},{14,12},{9,11},{1... | collective-permute-start | bytes 786440 | tf_op jit(solution)/shard_map/ppermute | solution.py:64
  48.7 6.2 %collective-permute-start.12 = (f32[256,256]{1,0:T(8,128)S(1)}, f32[256,256]{1,0:T(8,128)S(1)}, u32[]{:S(2)}, u32[]{:S(2)}) collective-permute-start(f32[256,256]{1,0:T(8,128)S(1)} %get-tuple-element.120), channel_id=1, source_target_pairs={{0,2},{6,4},{1,3},{4,6},{5,7},{8,10},{14,12},{9,11},{12,14},{13,15... | collective-permute-start | bytes 786440 | tf_op jit(solution)/shard_map/ppermute | solution.py:64
  55.8 4.0 %collective-permute-start.15 = (f32[256,256]{1,0:T(8,128)S(1)}, f32[256,256]{1,0:T(8,128)S(1)}, u32[]{:S(2)}, u32[]{:S(2)}) collective-permute-start(f32[256,256]{1,0:T(8,128)S(1)} %add_select_fusion.27), channel_id=1, source_target_pairs={{0,2},{6,4},{1,3},{7,5},{4,6},{2,0},{5,7},{8,10},{14,12},{9,11},{1... | collective-permute-start | bytes 786440 | tf_op jit(solution)/shard_map/ppermute | solution.py:64
  61.1 6.2 %collective-permute-start.17 = (f32[256,256]{1,0:T(8,128)S(1)}, f32[256,256]{1,0:T(8,128)S(1)}, u32[]{:S(2)}, u32[]{:S(2)}) collective-permute-start(f32[256,256]{1,0:T(8,128)S(1)} %add_select_fusion.26), channel_id=1, source_target_pairs={{0,2},{6,4},{1,3},{4,6},{5,7},{8,10},{14,12},{9,11},{12,14},{13,15... | collective-permute-start | bytes 786440 | tf_op jit(solution)/shard_map/ppermute | solution.py:64
  68.1 1.9 fusion.60
  70.9 4.6 %collective-permute-start.19 = (f32[256,256]{1,0:T(8,128)S(1)}, f32[256,256]{1,0:T(8,128)S(1)}, u32[]{:S(2)}, u32[]{:S(2)}) collective-permute-start(f32[256,256]{1,0:T(8,128)S(1)} %get-tuple-element.132), channel_id=1, source_target_pairs={{0,2},{6,4},{1,3},{7,5},{4,6},{2,0},{5,7},{8,10},{14,12},{9,11},{1... | collective-permute-start | bytes 786440 | tf_op jit(solution)/shard_map/ppermute | solution.py:64
  76.2 5.2 %collective-permute-start.21 = (f32[256,256]{1,0:T(8,128)S(1)}, f32[256,256]{1,0:T(8,128)S(1)}, u32[]{:S(2)}, u32[]{:S(2)}) collective-permute-start(f32[256,256]{1,0:T(8,128)S(1)} %get-tuple-element.136), channel_id=1, source_target_pairs={{0,2},{6,4},{1,3},{4,6},{5,7},{8,10},{14,12},{9,11},{12,14},{13,15... | collective-permute-start | bytes 786440 | tf_op jit(solution)/shard_map/ppermute | solution.py:64
  82.1 1.8 fusion.36
  84.2 4.0 %collective-permute-start.23 = (f32[256,256]{1,0:T(8,128)S(1)}, f32[256,256]{1,0:T(8,128)S(1)}, u32[]{:S(2)}, u32[]{:S(2)}) collective-permute-start(f32[256,256]{1,0:T(8,128)S(1)} %add_select_fusion.23), channel_id=1, source_target_pairs={{6,4},{0,2},{7,5},{4,6},{2,0},{5,7},{14,12},{8,10},{15,13},{12,14}... | collective-permute-start | bytes 786440 | tf_op jit(solution)/shard_map/ppermute | solution.py:64
  90.5 1.9 fusion.63
  93.5 10.9 %collective-permute-start.27 = (f32[256,256]{1,0:T(8,128)S(1)}, f32[256,256]{1,0:T(8,128)S(1)}, u32[]{:S(2)}, u32[]{:S(2)}) collective-permute-start(f32[256,256]{1,0:T(8,128)S(1)} %get-tuple-element.148), channel_id=1, source_target_pairs={{6,4},{0,2},{7,5},{4,6},{2,0},{5,7},{14,12},{8,10},{15,13},{12,14}... | collective-permute-start | bytes 786440 | tf_op jit(solution)/shard_map/ppermute | solution.py:64
  106.6 2.2 collective-permute-done.27
  108.8 1.9 fusion.39
  110.8 10.1 %collective-permute-start.32 = (f32[256,256]{1,0:T(8,128)S(1)}, f32[256,256]{1,0:T(8,128)S(1)}, u32[]{:S(2)}, u32[]{:S(2)}) collective-permute-start(f32[256,256]{1,0:T(8,128)S(1)} %add_select_fusion.19), channel_id=1, source_target_pairs={{6,4},{0,2},{7,5},{2,0},{4,6},{3,1},{5,7},{14,12},{8,10},{15,13},{... | collective-permute-start | bytes 786440 | tf_op jit(solution)/shard_map/ppermute | solution.py:64
  123.9 1.9 fusion.66
  126.5 1.5 collective-permute-done.32
  128.9 5.9 %collective-permute-start.36 = (f32[256,256]{1,0:T(8,128)S(1)}, f32[256,256]{1,0:T(8,128)S(1)}, u32[]{:S(2)}, u32[]{:S(2)}) collective-permute-start(f32[256,256]{1,0:T(8,128)S(1)} %get-tuple-element.164), channel_id=1, source_target_pairs={{6,4},{0,2},{7,5},{2,0},{4,6},{3,1},{5,7},{14,12},{8,10},{15,13},{... | collective-permute-start | bytes 786440 | tf_op jit(solution)/shard_map/ppermute | solution.py:64
  137.5 3.4 %collective-permute-done.36 = f32[256,256]{1,0:T(8,128)S(1)} collective-permute-done((f32[256,256]{1,0:T(8,128)S(1)}, f32[256,256]{1,0:T(8,128)S(1)}, u32[]{:S(2)}, u32[]{:S(2)}) %collective-permute-start.36) | collective-permute-done | bytes 262176 | tf_op jit(solution)/shard_map/ppermute | solution.py:64
  141.8 1.9 fusion.42
  143.7 6.9 %collective-permute-start.41 = (f32[256,256]{1,0:T(8,128)S(1)}, f32[256,256]{1,0:T(8,128)S(1)}, u32[]{:S(2)}, u32[]{:S(2)}) collective-permute-start(f32[256,256]{1,0:T(8,128)S(1)} %add_select_fusion.15), channel_id=1, source_target_pairs={{6,4},{0,2},{7,5},{2,0},{4,6},{3,1},{5,7},{14,12},{8,10},{15,13},{... | collective-permute-start | bytes 786440 | tf_op jit(solution)/shard_map/ppermute | solution.py:64
  157.1 8.3 %collective-permute-start.45 = (f32[256,256]{1,0:T(8,128)S(1)}, f32[256,256]{1,0:T(8,128)}, u32[]{:S(2)}, u32[]{:S(2)}) collective-permute-start(f32[256,256]{1,0:T(8,128)S(1)} %get-tuple-element.180), channel_id=1, source_target_pairs={{6,4},{0,2},{7,5},{2,0},{4,6},{3,1},{5,7},{14,12},{8,10},{15,13},{... | collective-permute-start | bytes 786440 | tf_op jit(solution)/shard_map/ppermute | solution.py:64
  165.4 1.4 collective-permute-start.46
  170.3 1.7 collective-permute-done.45
  172.9 1.8 fusion.150
  180.9 2.5 fusion.16
  184.1 2.2 collective-permute-done.49
  188.4 4.9 %collective-permute-done.51 = f32[256,256]{1,0:T(8,128)S(1)} collective-permute-done((f32[256,256]{1,0:T(8,128)S(1)}, f32[256,256]{1,0:T(8,128)S(1)}, u32[]{:S(2)}, u32[]{:S(2)}) %collective-permute-start.51) | collective-permute-done | bytes 262176 | tf_op jit(solution)/shard_map/ppermute | solution.py:64
  193.4 1.5 collective-permute-start.54
  195.7 3.5 %collective-permute-done.53 = f32[256,256]{1,0:T(8,128)S(1)} collective-permute-done((f32[256,256]{1,0:T(8,128)S(1)}, f32[256,256]{1,0:T(8,128)S(1)}, u32[]{:S(2)}, u32[]{:S(2)}) %collective-permute-start.53) | collective-permute-done | bytes 262176 | tf_op jit(solution)/shard_map/ppermute | solution.py:64
  200.0 2.0 collective-permute-done.54
  204.1 1.9 collective-permute-done.55
  206.1 1.6 collective-permute-start.56
  207.7 1.5 collective-permute-start.58
  209.2 5.3 %collective-permute-done.56 = f32[256,256]{1,0:T(8,128)S(1)} collective-permute-done((f32[256,256]{1,0:T(8,128)S(1)}, f32[256,256]{1,0:T(8,128)S(1)}, u32[]{:S(2)}, u32[]{:S(2)}) %collective-permute-start.56) | collective-permute-done | bytes 262176 | tf_op jit(solution)/shard_map/ppermute | solution.py:294
  216.4 1.5 collective-permute-start.57
  217.9 5.1 %collective-permute-done.59 = f32[256,256]{1,0:T(8,128)S(1)} collective-permute-done((f32[256,256]{1,0:T(8,128)S(1)}, f32[256,256]{1,0:T(8,128)S(1)}, u32[]{:S(2)}, u32[]{:S(2)}) %collective-permute-start.59) | collective-permute-done | bytes 262176 | tf_op jit(solution)/shard_map/ppermute | solution.py:297
  226.0 5.5 %collective-permute-done.61 = f32[256,128]{1,0:T(8,128)S(1)} collective-permute-done((f32[256,128]{1,0:T(8,128)S(1)}, f32[256,128]{1,0:T(8,128)S(1)}, u32[]{:S(2)}, u32[]{:S(2)}) %collective-permute-start.61) | collective-permute-done | bytes 131104 | tf_op jit(solution)/shard_map/ppermute | solution.py:317
  233.6 6.5 %collective-permute-done.62 = f32[256,128]{1,0:T(8,128)S(1)} collective-permute-done((f32[256,128]{1,0:T(8,128)S(1)}, f32[256,128]{1,0:T(8,128)S(1)}, u32[]{:S(2)}, u32[]{:S(2)}) %collective-permute-start.62) | collective-permute-done | bytes 131104 | tf_op jit(solution)/shard_map/ppermute | solution.py:317
  241.5 10.8 %whiten.1 = f32[1024,256]{1,0:T(8,128)} custom-call(f32[256,256]{1,0:T(8,128)S(1)} %pad_maximum_fusion.2.gram_ref, f32[1024,256]{1,0:T(8,128)S(1)} %pad_maximum_fusion.merged_ref), custom_call_target="tpu_custom_call" | custom-call | tf_op jit(solution)/shard_map/whiten/pallas_call | solution.py:182
  (222 shorter events, 62.0 us)
Async XLA Ops:
  5.2 11.9 %collective-permute-start = (f32[256,256]{1,0:T(8,128)}, f32[256,256]{1,0:T(8,128)S(1)}, u32[]{:S(2)}, u32[]{:S(2)}) collective-permute-start(f32[256,256]{1,0:T(8,128)} %get-tuple-element.250), channel_id=1, source_target_pairs={{0,2},{6,4},{1,3},{7,5},{8,10},{14,12},{9,11},{15,13},{16,18},{22,... | collective-permute-start | bytes 786440 | tf_op jit(solution)/shard_map/ppermute | solution.py:64
  10.1 12.8 %collective-permute-start.1 = (f32[256,256]{1,0:T(8,128)S(1)}, f32[256,256]{1,0:T(8,128)S(1)}, u32[]{:S(2)}, u32[]{:S(2)}) collective-permute-start(f32[256,256]{1,0:T(8,128)S(1)} %get-tuple-element.251), channel_id=1, source_target_pairs={{0,2},{6,4},{1,3},{8,10},{14,12},{9,11},{16,18},{22,20},{17,19},{2... | collective-permute-start | bytes 786440 | tf_op jit(solution)/shard_map/ppermute | solution.py:64
  17.2 11.1 %collective-permute-start.2 = (f32[256,256]{1,0:T(8,128)S(1)}, f32[256,256]{1,0:T(8,128)S(1)}, u32[]{:S(2)}, u32[]{:S(2)}) collective-permute-start(f32[256,256]{1,0:T(8,128)S(1)} %get-tuple-element.102), channel_id=1, source_target_pairs={{0,2},{6,4},{1,3},{7,5},{8,10},{14,12},{9,11},{15,13},{16,18},{22,... | collective-permute-start | bytes 786440 | tf_op jit(solution)/shard_map/ppermute | solution.py:64
  23.1 11.0 %collective-permute-start.4 = (f32[256,256]{1,0:T(8,128)S(1)}, f32[256,256]{1,0:T(8,128)S(1)}, u32[]{:S(2)}, u32[]{:S(2)}) collective-permute-start(f32[256,256]{1,0:T(8,128)S(1)} %get-tuple-element.104), channel_id=1, source_target_pairs={{0,2},{6,4},{1,3},{8,10},{14,12},{9,11},{16,18},{22,20},{17,19},{2... | collective-permute-start | bytes 786440 | tf_op jit(solution)/shard_map/ppermute | solution.py:64
  29.5 12.0 %collective-permute-start.6 = (f32[256,256]{1,0:T(8,128)S(1)}, f32[256,256]{1,0:T(8,128)S(1)}, u32[]{:S(2)}, u32[]{:S(2)}) collective-permute-start(f32[256,256]{1,0:T(8,128)S(1)} %get-tuple-element.108), channel_id=1, source_target_pairs={{0,2},{6,4},{1,3},{7,5},{4,6},{2,0},{5,7},{8,10},{14,12},{9,11},{1... | collective-permute-start | bytes 786440 | tf_op jit(solution)/shard_map/ppermute | solution.py:64
  34.1 7.5 %collective-permute-start.7 = (f32[256,256]{1,0:T(8,128)S(1)}, f32[256,256]{1,0:T(8,128)S(1)}, u32[]{:S(2)}, u32[]{:S(2)}) collective-permute-start(f32[256,256]{1,0:T(8,128)S(1)} %get-tuple-element.113), channel_id=1, source_target_pairs={{2,4},{4,2},{3,5},{10,12},{12,10},{11,13},{18,20},{20,18},{19,21},... | collective-permute-start | bytes 786440 | tf_op jit(solution)/shard_map/ppermute | solution.py:66
  35.8 12.1 %collective-permute-start.8 = (f32[256,256]{1,0:T(8,128)S(1)}, f32[256,256]{1,0:T(8,128)S(1)}, u32[]{:S(2)}, u32[]{:S(2)}) collective-permute-start(f32[256,256]{1,0:T(8,128)S(1)} %add_select_fusion.30), channel_id=1, source_target_pairs={{0,2},{6,4},{1,3},{4,6},{5,7},{8,10},{14,12},{9,11},{12,14},{13,15... | collective-permute-start | bytes 786440 | tf_op jit(solution)/shard_map/ppermute | solution.py:64
  42.7 12.9 %collective-permute-start.10 = (f32[256,256]{1,0:T(8,128)S(1)}, f32[256,256]{1,0:T(8,128)S(1)}, u32[]{:S(2)}, u32[]{:S(2)}) collective-permute-start(f32[256,256]{1,0:T(8,128)S(1)} %get-tuple-element.116), channel_id=1, source_target_pairs={{0,2},{6,4},{1,3},{7,5},{4,6},{2,0},{5,7},{8,10},{14,12},{9,11},{1... | collective-permute-start | bytes 786440 | tf_op jit(solution)/shard_map/ppermute | solution.py:64
  47.9 7.7 %collective-permute-start.11 = (f32[256,256]{1,0:T(8,128)S(1)}, f32[256,256]{1,0:T(8,128)S(1)}, u32[]{:S(2)}, u32[]{:S(2)}) collective-permute-start(f32[256,256]{1,0:T(8,128)S(1)} %get-tuple-element.121), channel_id=1, source_target_pairs={{2,4},{4,2},{3,5},{10,12},{12,10},{11,13},{18,20},{20,18},{19,21},... | collective-permute-start | bytes 786440 | tf_op jit(solution)/shard_map/ppermute | solution.py:66
  48.7 11.5 %collective-permute-start.12 = (f32[256,256]{1,0:T(8,128)S(1)}, f32[256,256]{1,0:T(8,128)S(1)}, u32[]{:S(2)}, u32[]{:S(2)}) collective-permute-start(f32[256,256]{1,0:T(8,128)S(1)} %get-tuple-element.120), channel_id=1, source_target_pairs={{0,2},{6,4},{1,3},{4,6},{5,7},{8,10},{14,12},{9,11},{12,14},{13,15... | collective-permute-start | bytes 786440 | tf_op jit(solution)/shard_map/ppermute | solution.py:64
  55.8 14.9 %collective-permute-start.15 = (f32[256,256]{1,0:T(8,128)S(1)}, f32[256,256]{1,0:T(8,128)S(1)}, u32[]{:S(2)}, u32[]{:S(2)}) collective-permute-start(f32[256,256]{1,0:T(8,128)S(1)} %add_select_fusion.27), channel_id=1, source_target_pairs={{0,2},{6,4},{1,3},{7,5},{4,6},{2,0},{5,7},{8,10},{14,12},{9,11},{1... | collective-permute-start | bytes 786440 | tf_op jit(solution)/shard_map/ppermute | solution.py:64
  60.4 10.3 %collective-permute-start.16 = (f32[256,256]{1,0:T(8,128)S(1)}, f32[256,256]{1,0:T(8,128)S(1)}, u32[]{:S(2)}, u32[]{:S(2)}) collective-permute-start(f32[256,256]{1,0:T(8,128)S(1)} %get-tuple-element.129), channel_id=1, source_target_pairs={{2,4},{4,2},{3,5},{10,12},{12,10},{11,13},{18,20},{20,18},{19,21},... | collective-permute-start | bytes 786440 | tf_op jit(solution)/shard_map/ppermute | solution.py:66
  61.1 14.3 %collective-permute-start.17 = (f32[256,256]{1,0:T(8,128)S(1)}, f32[256,256]{1,0:T(8,128)S(1)}, u32[]{:S(2)}, u32[]{:S(2)}) collective-permute-start(f32[256,256]{1,0:T(8,128)S(1)} %add_select_fusion.26), channel_id=1, source_target_pairs={{0,2},{6,4},{1,3},{4,6},{5,7},{8,10},{14,12},{9,11},{12,14},{13,15... | collective-permute-start | bytes 786440 | tf_op jit(solution)/shard_map/ppermute | solution.py:64
  67.3 8.1 %collective-permute-start.18 = (f32[256,256]{1,0:T(8,128)S(1)}, f32[256,256]{1,0:T(8,128)S(1)}, u32[]{:S(2)}, u32[]{:S(2)}) collective-permute-start(f32[256,256]{1,0:T(8,128)S(1)} %get-tuple-element.133), channel_id=1, source_target_pairs={{2,4},{4,2},{3,5},{10,12},{12,10},{11,13},{18,20},{20,18},{19,21},... | collective-permute-start | bytes 786440 | tf_op jit(solution)/shard_map/ppermute | solution.py:66
  70.0 12.1 %collective-permute-start.14 = (f32[512,256]{0,1:T(8,128)S(1)}, f32[512,256]{0,1:T(8,128)S(1)}, u32[]{:S(2)}, u32[]{:S(2)}) collective-permute-start(f32[512,256]{0,1:T(8,128)S(1)} %fusion.60), channel_id=1, source_target_pairs={{4,5},{5,4},{6,7},{7,6},{12,13},{13,12},{14,15},{15,14},{20,21},{2... | collective-permute-start | bytes 1572872 | tf_op jit(solution)/shard_map/ppermute | solution.py:234
  70.9 13.1 %collective-permute-start.19 = (f32[256,256]{1,0:T(8,128)S(1)}, f32[256,256]{1,0:T(8,128)S(1)}, u32[]{:S(2)}, u32[]{:S(2)}) collective-permute-start(f32[256,256]{1,0:T(8,128)S(1)} %get-tuple-element.132), channel_id=1, source_target_pairs={{0,2},{6,4},{1,3},{7,5},{4,6},{2,0},{5,7},{8,10},{14,12},{9,11},{1... | collective-permute-start | bytes 786440 | tf_op jit(solution)/shard_map/ppermute | solution.py:64
  75.6 8.4 %collective-permute-start.20 = (f32[256,256]{1,0:T(8,128)S(1)}, f32[256,256]{1,0:T(8,128)S(1)}, u32[]{:S(2)}, u32[]{:S(2)}) collective-permute-start(f32[256,256]{1,0:T(8,128)S(1)} %get-tuple-element.137), channel_id=1, source_target_pairs={{2,4},{4,2},{3,5},{10,12},{12,10},{11,13},{18,20},{20,18},{19,21},... | collective-permute-start | bytes 786440 | tf_op jit(solution)/shard_map/ppermute | solution.py:66
  76.2 12.0 %collective-permute-start.21 = (f32[256,256]{1,0:T(8,128)S(1)}, f32[256,256]{1,0:T(8,128)S(1)}, u32[]{:S(2)}, u32[]{:S(2)}) collective-permute-start(f32[256,256]{1,0:T(8,128)S(1)} %get-tuple-element.136), channel_id=1, source_target_pairs={{0,2},{6,4},{1,3},{4,6},{5,7},{8,10},{14,12},{9,11},{12,14},{13,15... | collective-permute-start | bytes 786440 | tf_op jit(solution)/shard_map/ppermute | solution.py:64
  84.2 9.2 %collective-permute-start.23 = (f32[256,256]{1,0:T(8,128)S(1)}, f32[256,256]{1,0:T(8,128)S(1)}, u32[]{:S(2)}, u32[]{:S(2)}) collective-permute-start(f32[256,256]{1,0:T(8,128)S(1)} %add_select_fusion.23), channel_id=1, source_target_pairs={{6,4},{0,2},{7,5},{4,6},{2,0},{5,7},{14,12},{8,10},{15,13},{12,14}... | collective-permute-start | bytes 786440 | tf_op jit(solution)/shard_map/ppermute | solution.py:64
  89.2 15.3 %collective-permute-start.25 = (f32[256,256]{1,0:T(8,128)S(1)}, f32[256,256]{1,0:T(8,128)S(1)}, u32[]{:S(2)}, u32[]{:S(2)}) collective-permute-start(f32[256,256]{1,0:T(8,128)S(1)} %add_select_fusion.22), channel_id=1, source_target_pairs={{6,4},{7,5},{4,6},{5,7},{14,12},{15,13},{12,14},{13,15},{22,20},{2... | collective-permute-start | bytes 786440 | tf_op jit(solution)/shard_map/ppermute | solution.py:64
  89.8 14.6 %collective-permute-start.26 = (f32[256,256]{1,0:T(8,128)S(1)}, f32[256,256]{1,0:T(8,128)S(1)}, u32[]{:S(2)}, u32[]{:S(2)}) collective-permute-start(f32[256,256]{1,0:T(8,128)S(1)} %get-tuple-element.149), channel_id=1, source_target_pairs={{2,4},{4,2},{3,5},{10,12},{12,10},{11,13},{18,20},{20,18},{19,21},... | collective-permute-start | bytes 786440 | tf_op jit(solution)/shard_map/ppermute | solution.py:66
  92.5 16.3 %collective-permute-start.29 = (f32[512,256]{0,1:T(8,128)S(1)}, f32[512,256]{0,1:T(8,128)S(1)}, u32[]{:S(2)}, u32[]{:S(2)}) collective-permute-start(f32[512,256]{0,1:T(8,128)S(1)} %fusion.63), channel_id=1, source_target_pairs={{4,5},{5,4},{6,7},{7,6},{12,13},{13,12},{14,15},{15,14},{20,21},{2... | collective-permute-start | bytes 1572872 | tf_op jit(solution)/shard_map/ppermute | solution.py:234
  93.5 15.3 %collective-permute-start.27 = (f32[256,256]{1,0:T(8,128)S(1)}, f32[256,256]{1,0:T(8,128)S(1)}, u32[]{:S(2)}, u32[]{:S(2)}) collective-permute-start(f32[256,256]{1,0:T(8,128)S(1)} %get-tuple-element.148), channel_id=1, source_target_pairs={{6,4},{0,2},{7,5},{4,6},{2,0},{5,7},{14,12},{8,10},{15,13},{12,14}... | collective-permute-start | bytes 786440 | tf_op jit(solution)/shard_map/ppermute | solution.py:64
  105.2 15.7 %collective-permute-start.30 = (f32[256,256]{1,0:T(8,128)S(1)}, f32[256,256]{1,0:T(8,128)S(1)}, u32[]{:S(2)}, u32[]{:S(2)}) collective-permute-start(f32[256,256]{1,0:T(8,128)S(1)} %get-tuple-element.152), channel_id=1, source_target_pairs={{6,4},{7,5},{4,6},{5,7},{14,12},{15,13},{12,14},{13,15},{22,20},{2... | collective-permute-start | bytes 786440 | tf_op jit(solution)/shard_map/ppermute | solution.py:64
  105.9 15.0 %collective-permute-start.31 = (f32[256,256]{1,0:T(8,128)S(1)}, f32[256,256]{1,0:T(8,128)S(1)}, u32[]{:S(2)}, u32[]{:S(2)}) collective-permute-start(f32[256,256]{1,0:T(8,128)S(1)} %get-tuple-element.157), channel_id=1, source_target_pairs={{4,2},{2,4},{5,3},{12,10},{10,12},{13,11},{20,18},{18,20},{21,19},... | collective-permute-start | bytes 786440 | tf_op jit(solution)/shard_map/ppermute | solution.py:66
  110.8 17.2 %collective-permute-start.32 = (f32[256,256]{1,0:T(8,128)S(1)}, f32[256,256]{1,0:T(8,128)S(1)}, u32[]{:S(2)}, u32[]{:S(2)}) collective-permute-start(f32[256,256]{1,0:T(8,128)S(1)} %add_select_fusion.19), channel_id=1, source_target_pairs={{6,4},{0,2},{7,5},{2,0},{4,6},{3,1},{5,7},{14,12},{8,10},{15,13},{... | collective-permute-start | bytes 786440 | tf_op jit(solution)/shard_map/ppermute | solution.py:64
  121.9 12.9 %collective-permute-start.34 = (f32[256,256]{1,0:T(8,128)S(1)}, f32[256,256]{1,0:T(8,128)S(1)}, u32[]{:S(2)}, u32[]{:S(2)}) collective-permute-start(f32[256,256]{1,0:T(8,128)S(1)} %add_select_fusion.18), channel_id=1, source_target_pairs={{6,4},{7,5},{2,0},{4,6},{3,1},{14,12},{15,13},{10,8},{12,14},{11,9... | collective-permute-start | bytes 786440 | tf_op jit(solution)/shard_map/ppermute | solution.py:64
  123.2 11.6 %collective-permute-start.35 = (f32[256,256]{1,0:T(8,128)S(1)}, f32[256,256]{1,0:T(8,128)S(1)}, u32[]{:S(2)}, u32[]{:S(2)}) collective-permute-start(f32[256,256]{1,0:T(8,128)S(1)} %get-tuple-element.165), channel_id=1, source_target_pairs={{4,2},{2,4},{5,3},{12,10},{10,12},{13,11},{20,18},{18,20},{21,19},... | collective-permute-start | bytes 786440 | tf_op jit(solution)/shard_map/ppermute | solution.py:66
  125.8 15.9 %collective-permute-start.38 = (f32[512,256]{0,1:T(8,128)S(1)}, f32[512,256]{0,1:T(8,128)S(1)}, u32[]{:S(2)}, u32[]{:S(2)}) collective-permute-start(f32[512,256]{0,1:T(8,128)S(1)} %fusion.66), channel_id=1, source_target_pairs={{4,5},{5,4},{6,7},{7,6},{12,13},{13,12},{14,15},{15,14},{20,21},{2... | collective-permute-start | bytes 1572872 | tf_op jit(solution)/shard_map/ppermute | solution.py:234
  128.9 12.1 %collective-permute-start.36 = (f32[256,256]{1,0:T(8,128)S(1)}, f32[256,256]{1,0:T(8,128)S(1)}, u32[]{:S(2)}, u32[]{:S(2)}) collective-permute-start(f32[256,256]{1,0:T(8,128)S(1)} %get-tuple-element.164), channel_id=1, source_target_pairs={{6,4},{0,2},{7,5},{2,0},{4,6},{3,1},{5,7},{14,12},{8,10},{15,13},{... | collective-permute-start | bytes 786440 | tf_op jit(solution)/shard_map/ppermute | solution.py:64
  135.5 15.1 %collective-permute-start.39 = (f32[256,256]{1,0:T(8,128)S(1)}, f32[256,256]{1,0:T(8,128)S(1)}, u32[]{:S(2)}, u32[]{:S(2)}) collective-permute-start(f32[256,256]{1,0:T(8,128)S(1)} %get-tuple-element.168), channel_id=1, source_target_pairs={{6,4},{7,5},{2,0},{4,6},{3,1},{14,12},{15,13},{10,8},{12,14},{11,9... | collective-permute-start | bytes 786440 | tf_op jit(solution)/shard_map/ppermute | solution.py:64
  136.8 13.8 %collective-permute-start.40 = (f32[256,256]{1,0:T(8,128)S(1)}, f32[256,256]{1,0:T(8,128)S(1)}, u32[]{:S(2)}, u32[]{:S(2)}) collective-permute-start(f32[256,256]{1,0:T(8,128)S(1)} %get-tuple-element.173), channel_id=1, source_target_pairs={{4,2},{2,4},{5,3},{12,10},{10,12},{13,11},{20,18},{18,20},{21,19},... | collective-permute-start | bytes 786440 | tf_op jit(solution)/shard_map/ppermute | solution.py:66
  143.7 12.5 %collective-permute-start.41 = (f32[256,256]{1,0:T(8,128)S(1)}, f32[256,256]{1,0:T(8,128)S(1)}, u32[]{:S(2)}, u32[]{:S(2)}) collective-permute-start(f32[256,256]{1,0:T(8,128)S(1)} %add_select_fusion.15), channel_id=1, source_target_pairs={{6,4},{0,2},{7,5},{2,0},{4,6},{3,1},{5,7},{14,12},{8,10},{15,13},{... | collective-permute-start | bytes 786440 | tf_op jit(solution)/shard_map/ppermute | solution.py:64
  152.2 13.2 %collective-permute-start.43 = (f32[256,256]{1,0:T(8,128)S(1)}, f32[256,256]{1,0:T(8,128)S(1)}, u32[]{:S(2)}, u32[]{:S(2)}) collective-permute-start(f32[256,256]{1,0:T(8,128)S(1)} %add_select_fusion.14), channel_id=1, source_target_pairs={{6,4},{7,5},{2,0},{4,6},{3,1},{14,12},{15,13},{10,8},{12,14},{11,9... | collective-permute-start | bytes 786440 | tf_op jit(solution)/shard_map/ppermute | solution.py:64
  153.5 11.9 %collective-permute-start.44 = (f32[256,256]{1,0:T(8,128)S(1)}, f32[256,256]{1,0:T(8,128)S(1)}, u32[]{:S(2)}, u32[]{:S(2)}) collective-permute-start(f32[256,256]{1,0:T(8,128)S(1)} %get-tuple-element.181), channel_id=1, source_target_pairs={{4,2},{2,4},{5,3},{12,10},{10,12},{13,11},{20,18},{18,20},{21,19},... | collective-permute-start | bytes 786440 | tf_op jit(solution)/shard_map/ppermute | solution.py:66
  157.1 14.9 %collective-permute-start.45 = (f32[256,256]{1,0:T(8,128)S(1)}, f32[256,256]{1,0:T(8,128)}, u32[]{:S(2)}, u32[]{:S(2)}) collective-permute-start(f32[256,256]{1,0:T(8,128)S(1)} %get-tuple-element.180), channel_id=1, source_target_pairs={{6,4},{0,2},{7,5},{2,0},{4,6},{3,1},{5,7},{14,12},{8,10},{15,13},{... | collective-permute-start | bytes 786440 | tf_op jit(solution)/shard_map/ppermute | solution.py:64
  167.6 8.4 %collective-permute-start.47 = (f32[256,256]{1,0:T(8,128)S(1)}, f32[256,256]{1,0:T(8,128)}, u32[]{:S(2)}, u32[]{:S(2)}) collective-permute-start(f32[256,256]{1,0:T(8,128)S(1)} %get-tuple-element.184), channel_id=1, source_target_pairs={{6,4},{7,5},{2,0},{4,6},{3,1},{14,12},{15,13},{10,8},{12,14},{11,9... | collective-permute-start | bytes 786440 | tf_op jit(solution)/shard_map/ppermute | solution.py:64
  174.7 11.6 %collective-permute-start.49 = (f32[256,256]{1,0:T(8,128)S(1)}, f32[256,256]{1,0:T(8,128)S(1)}, u32[]{:S(2)}, u32[]{:S(2)}) collective-permute-start(f32[256,256]{1,0:T(8,128)S(1)} %add.305), channel_id=1, source_target_pairs={{2,0},{4,6},{3,1},{5,7},{10,8},{12,14},{11,9},{13,15},{18,16},{20,... | collective-permute-start | bytes 786440 | tf_op jit(solution)/shard_map/ppermute | solution.py:64
  178.2 8.1 %collective-permute-start.50 = (f32[256,256]{1,0:T(8,128)S(1)}, f32[256,256]{1,0:T(8,128)S(1)}, u32[]{:S(2)}, u32[]{:S(2)}) collective-permute-start(f32[256,256]{1,0:T(8,128)S(1)} %get-tuple-element.193), channel_id=1, source_target_pairs={{4,2},{2,4},{5,3},{12,10},{10,12},{13,11},{20,18},{18,20},{21,19},... | collective-permute-start | bytes 786440 | tf_op jit(solution)/shard_map/ppermute | solution.py:66
  178.9 14.4 %collective-permute-start.51 = (f32[256,256]{1,0:T(8,128)S(1)}, f32[256,256]{1,0:T(8,128)S(1)}, u32[]{:S(2)}, u32[]{:S(2)}) collective-permute-start(f32[256,256]{1,0:T(8,128)S(1)} %add.308), channel_id=1, source_target_pairs={{2,0},{4,6},{3,1},{10,8},{12,14},{11,9},{18,16},{20,22},{19,17},{2... | collective-permute-start | bytes 786440 | tf_op jit(solution)/shard_map/ppermute | solution.py:64
  180.2 13.1 %collective-permute-start.52 = (f32[256,256]{1,0:T(8,128)S(1)}, f32[256,256]{1,0:T(8,128)S(1)}, u32[]{:S(2)}, u32[]{:S(2)}) collective-permute-start(f32[256,256]{1,0:T(8,128)S(1)} %get-tuple-element.196), channel_id=1, source_target_pairs={{4,2},{2,4},{5,3},{12,10},{10,12},{13,11},{20,18},{18,20},{21,19},... | collective-permute-start | bytes 786440 | tf_op jit(solution)/shard_map/ppermute | solution.py:66
  186.4 12.8 %collective-permute-start.53 = (f32[256,256]{1,0:T(8,128)S(1)}, f32[256,256]{1,0:T(8,128)S(1)}, u32[]{:S(2)}, u32[]{:S(2)}) collective-permute-start(f32[256,256]{1,0:T(8,128)S(1)} %add.310), channel_id=1, source_target_pairs={{2,0},{4,6},{3,1},{5,7},{10,8},{12,14},{11,9},{13,15},{18,16},{20,... | collective-permute-start | bytes 786440 | tf_op jit(solution)/shard_map/ppermute | solution.py:64
  193.4 8.7 %collective-permute-start.54 = (f32[256,256]{1,0:T(8,128)S(1)}, f32[256,256]{1,0:T(8,128)S(1)}, u32[]{:S(2)}, u32[]{:S(2)}) collective-permute-start(f32[256,256]{1,0:T(8,128)S(1)} %add.311), channel_id=1, source_target_pairs={{2,0},{4,6},{3,1},{10,8},{12,14},{11,9},{18,16},{20,22},{19,17},{2... | collective-permute-start | bytes 786440 | tf_op jit(solution)/shard_map/ppermute | solution.py:64
  206.1 8.4 %collective-permute-start.56 = (f32[256,256]{1,0:T(8,128)S(1)}, f32[256,256]{1,0:T(8,128)S(1)}, u32[]{:S(2)}, u32[]{:S(2)}) collective-permute-start(f32[256,256]{1,0:T(8,128)S(1)} %get-tuple-element.266), channel_id=1, source_target_pairs={{0,8},{8,0},{16,24},{24,16},{1,9},{9,1},{17,25},{25,17},{2,10},{10... | collective-permute-start | bytes 786440 | tf_op jit(solution)/shard_map/ppermute | solution.py:294
  207.7 8.1 %collective-permute-start.58 = (f32[256,256]{1,0:T(8,128)S(1)}, f32[256,256]{1,0:T(8,128)S(1)}, u32[]{:S(2)}, u32[]{:S(2)}) collective-permute-start(f32[256,256]{1,0:T(8,128)S(1)} %get-tuple-element.267), channel_id=1, source_target_pairs={{0,16},{8,24},{16,0},{24,8},{1,17},{9,25},{17,1},{25,9},{2,18},{10... | collective-permute-start | bytes 786440 | tf_op jit(solution)/shard_map/ppermute | solution.py:295
  215.8 7.3 %collective-permute-start.59 = (f32[256,256]{1,0:T(8,128)S(1)}, f32[256,256]{1,0:T(8,128)S(1)}, u32[]{:S(2)}, u32[]{:S(2)}) collective-permute-start(f32[256,256]{1,0:T(8,128)S(1)} %get-tuple-element.265), channel_id=1, source_target_pairs={{0,8},{8,0},{16,24},{24,16},{1,9},{9,1},{17,25},{25,17},{2,10},{10... | collective-permute-start | bytes 786440 | tf_op jit(solution)/shard_map/ppermute | solution.py:297
  224.6 15.5 %collective-permute-start.64 = (f32[512,256]{1,0:T(8,128)S(1)}, f32[512,256]{1,0:T(8,128)S(1)}, u32[]{:S(2)}, u32[]{:S(2)}) collective-permute-start(f32[512,256]{1,0:T(8,128)S(1)} %pad_maximum_fusion.1), channel_id=1, source_target_pairs={{0,1},{1,0},{2,3},{3,2},{4,5},{5,4},{6,7},{7,6},{8,9},{9,8},{10,11... | collective-permute-start | bytes 1572872 | tf_op jit(solution)/shard_map/ppermute | solution.py:299
  231.6 8.5 %collective-permute-start.62 = (f32[256,128]{1,0:T(8,128)S(1)}, f32[256,128]{1,0:T(8,128)S(1)}, u32[]{:S(2)}, u32[]{:S(2)}) collective-permute-start(f32[256,128]{1,0:T(8,128)S(1)} %add.324), channel_id=1, source_target_pairs={{0,4},{2,6},{4,0},{6,2},{1,5},{3,7},{5,1},{7,3},{8,12},{10,14},{12... | collective-permute-start | bytes 393224 | tf_op jit(solution)/shard_map/ppermute | solution.py:317
  (45 other events, 824.9 us)
where the time goes:
time: 254 us; the launch traced here: 252 us
  starting transfers between devices  141 us (56%)
  waiting for transfers between devices  51.2 us (20%)
  matrix products  23.1 us (9%)
  other arithmetic  17.1 us (7%)
  Pallas kernels  10.8 us (4%)
  local copies, waits for them, and re-layouts  7.18 us (3%)
    ppermute x28, starting transfers between devices, step(): ends_in = lax.ppermute(ends, axes, perm)  114 us
    ppermute x28, waiting for transfers between devices, step(): ends_in = lax.ppermute(ends, axes, perm)  23.4 us
    ppermute x24, starting transfers between devices, step(): pair_in = lax.ppermute(pair, axes, self.pairs_of(middle, 1))  18.4 us
    ppermute x2, waiting for transfers between devices, shards(): lax.ppermute(gram, 'sent', [(s, s ^ bit) for s in range(sent_size)])  12 us
    pallas_call x1, Pallas kernels, whiten(): pl.pallas_call(functools.partial(whiten_kernel, scale), out_shape=jax.Sha...  10.8 us
    another operation x9, other arithmetic  8.05 us
    dot_general x3, matrix products, term_of(): lax.dot_general(features, shared, down, preferred_element_type=jnp.float32)  6.82 us
    dot_general x3, matrix products, first_half(): half_part = jnp.dot(inv_factor[j], proj, precision=high)  5.81 us
  transfers between devices with their start and end apart: 65, of which 21 were waited for; matrix products, arithmetic and copies ran while one was open for 16% of the time, Pallas kernels for 0%

commit v1 on v0

--- a/solution.py
+++ b/solution.py
@@ -210,7 +210,7 @@
 
     chunk = CHUNK if use_line else col_half
     per_view = col_half // chunk
-    order = [q + h for q in range(per_view // 2) for h in (0, per_view // 2)] or [0]
+    order = [q + h for q in range(per_view // 2) for h in (per_view // 2, 0)] or [0]
     back_order = sorted(range(per_view), key=order.__getitem__)
     slots = [(j, q) for j in range(view_count) for q in order]
     firsts = [

time: 254 us -> 253 us (level)
  other arithmetic: 17.1 us -> 8.57 us
  waiting for transfers between devices: 51.2 us -> 58.4 us
  starting transfers between devices: 141 us -> 146 us
  local copies, waits for them, and re-layouts: 7.18 us -> 4.37 us
    ppermute x28, starting transfers between devices: 114 us -> 121 us  [step(): ends_in = lax.ppermute(ends, axes, perm)]
    another operation x9, other arithmetic: 8.05 us -> 1.19 us
    ppermute x28, waiting for transfers between devices: 23.4 us -> 29.2 us  [step(): ends_in = lax.ppermute(ends, axes, perm)]
    ppermute x1, waiting for transfers between devices: 0.29 us -> 5.15 us  [shards(): upper = upper + lax.ppermute(upper, 'view', near(2))]
    ppermute x1, waiting for transfers between devices: 5.13 us -> 1.19 us  [shards(): lower_part = lower_part + lax.ppermute(lower_part, 'view', near(1))]
  transfers between devices with their start and end apart: 65 -> 65, of which waited for: 21 -> 21; matrix products, arithmetic and copies ran while one was open for 16% -> 10% of each run, Pallas kernels for 0% -> 0%
where the time goes in v1:
time: 253 us; the launch traced here: 251 us
  starting transfers between devices  146 us (58%)
  waiting for transfers between devices  58.4 us (23%)
  matrix products  21.3 us (8%)
  Pallas kernels  10.8 us (4%)
  other arithmetic  8.57 us (3%)
  local copies, waits for them, and re-layouts  4.37 us (2%)
    ppermute x28, starting transfers between devices, step(): ends_in = lax.ppermute(ends, axes, perm)  121 us
    ppermute x28, waiting for transfers between devices, step(): ends_in = lax.ppermute(ends, axes, perm)  29.2 us
    ppermute x24, starting transfers between devices, step(): pair_in = lax.ppermute(pair, axes, self.pairs_of(middle, 1))  16.9 us
    ppermute x2, waiting for transfers between devices, shards(): lax.ppermute(gram, 'sent', [(s, s ^ bit) for s in range(sent_size)])  12.5 us
    pallas_call x1, Pallas kernels, whiten(): pl.pallas_call(functools.partial(whiten_kernel, scale), out_shape=jax.Sha...  10.8 us
    dot_general x3, matrix products, term_of(): lax.dot_general(features, shared, down, preferred_element_type=jnp.float32)  6.82 us
    dot_general x3, matrix products, first_half(): half_part = jnp.dot(inv_factor[j], proj, precision=high)  5.81 us
    dot_general x3, matrix products, back_terms(): lax.dot_general(inv_factor[j], first_half(proj, j), down, precision=high,...  5.5 us
  transfers between devices with their start and end apart: 65, of which 21 were waited for; matrix products, arithmetic and copies ran while one was open for 10% of the time, Pallas kernels for 0%

profile of v1, /device:TPU:0, one launch (start us, length us, event | category | flops | bytes accessed | tf_op | source)
XLA Modules:
  0.0 251.5 jit_solution(6467034591640110431)
XLA Ops:
  1.7 2.8 %fusion.45 = f32[1024,256]{1,0:T(8,128)S(1)} fusion(bf16[1024,256]{1,0:T(8,128)(2,1)S(1)} %copy-done, bf16[3,1024,1024]{2,1,0:T(8,128)(2,1)} %param.4), kind=kOutput, calls=%fused_computation.39 | convolution fusion | flops 537133056 | bytes 3670016 | tf_op jit(solution)/shard_map/dot_general | solution.py:243
  5.2 5.6 %collective-permute-start = (f32[256,256]{1,0:T(8,128)S(1)}, f32[256,256]{1,0:T(8,128)}, u32[]{:S(2)}, u32[]{:S(2)}) collective-permute-start(f32[256,256]{1,0:T(8,128)S(1)} %get-tuple-element.249), channel_id=1, source_target_pairs={{0,2},{6,4},{1,3},{8,10},{14,12},{9,11},{16,18},{22,20},{17,19},{2... | collective-permute-start | bytes 786440 | tf_op jit(solution)/shard_map/ppermute | solution.py:64
  12.1 1.7 fusion.54
  13.9 2.3 fusion.57
  17.8 5.2 %collective-permute-start.2 = (f32[256,256]{1,0:T(8,128)S(1)}, f32[256,256]{1,0:T(8,128)}, u32[]{:S(2)}, u32[]{:S(2)}) collective-permute-start(f32[256,256]{1,0:T(8,128)S(1)} %get-tuple-element.102), channel_id=1, source_target_pairs={{0,2},{6,4},{1,3},{8,10},{14,12},{9,11},{16,18},{22,20},{17,19},{2... | collective-permute-start | bytes 786440 | tf_op jit(solution)/shard_map/ppermute | solution.py:64
  23.0 1.4 collective-permute-start.3
  24.5 2.5 collective-permute-start.4
  27.7 1.3 collective-permute-done.2
  29.0 1.3 add_select_fusion.31
  30.3 4.6 %collective-permute-start.6 = (f32[256,256]{1,0:T(8,128)S(1)}, f32[256,256]{1,0:T(8,128)S(1)}, u32[]{:S(2)}, u32[]{:S(2)}) collective-permute-start(f32[256,256]{1,0:T(8,128)S(1)} %get-tuple-element.108), channel_id=1, source_target_pairs={{0,2},{6,4},{1,3},{4,6},{5,7},{8,10},{14,12},{9,11},{12,14},{13,15... | collective-permute-start | bytes 786440 | tf_op jit(solution)/shard_map/ppermute | solution.py:64
  36.7 5.5 %collective-permute-start.8 = (f32[256,256]{1,0:T(8,128)S(1)}, f32[256,256]{1,0:T(8,128)S(1)}, u32[]{:S(2)}, u32[]{:S(2)}) collective-permute-start(f32[256,256]{1,0:T(8,128)S(1)} %add_select_fusion.30), channel_id=1, source_target_pairs={{0,2},{6,4},{1,3},{7,5},{4,6},{2,0},{5,7},{8,10},{14,12},{9,11},{1... | collective-permute-start | bytes 786440 | tf_op jit(solution)/shard_map/ppermute | solution.py:64
  44.1 4.8 %collective-permute-start.10 = (f32[256,256]{1,0:T(8,128)S(1)}, f32[256,256]{1,0:T(8,128)S(1)}, u32[]{:S(2)}, u32[]{:S(2)}) collective-permute-start(f32[256,256]{1,0:T(8,128)S(1)} %get-tuple-element.116), channel_id=1, source_target_pairs={{0,2},{6,4},{1,3},{4,6},{5,7},{8,10},{14,12},{9,11},{12,14},{13,15... | collective-permute-start | bytes 786440 | tf_op jit(solution)/shard_map/ppermute | solution.py:64
  49.7 6.1 %collective-permute-start.12 = (f32[256,256]{1,0:T(8,128)S(1)}, f32[256,256]{1,0:T(8,128)S(1)}, u32[]{:S(2)}, u32[]{:S(2)}) collective-permute-start(f32[256,256]{1,0:T(8,128)S(1)} %get-tuple-element.120), channel_id=1, source_target_pairs={{0,2},{6,4},{1,3},{7,5},{4,6},{2,0},{5,7},{8,10},{14,12},{9,11},{1... | collective-permute-start | bytes 786440 | tf_op jit(solution)/shard_map/ppermute | solution.py:64
  56.8 4.7 %collective-permute-start.15 = (f32[256,256]{1,0:T(8,128)S(1)}, f32[256,256]{1,0:T(8,128)S(1)}, u32[]{:S(2)}, u32[]{:S(2)}) collective-permute-start(f32[256,256]{1,0:T(8,128)S(1)} %add_select_fusion.27), channel_id=1, source_target_pairs={{0,2},{6,4},{1,3},{4,6},{5,7},{8,10},{14,12},{9,11},{12,14},{13,15... | collective-permute-start | bytes 786440 | tf_op jit(solution)/shard_map/ppermute | solution.py:64
  62.4 7.1 %collective-permute-start.17 = (f32[256,256]{1,0:T(8,128)S(1)}, f32[256,256]{1,0:T(8,128)S(1)}, u32[]{:S(2)}, u32[]{:S(2)}) collective-permute-start(f32[256,256]{1,0:T(8,128)S(1)} %add_select_fusion.26), channel_id=1, source_target_pairs={{0,2},{6,4},{1,3},{7,5},{4,6},{2,0},{5,7},{8,10},{14,12},{9,11},{1... | collective-permute-start | bytes 786440 | tf_op jit(solution)/shard_map/ppermute | solution.py:64
  70.2 1.9 fusion.60
  73.0 3.8 %collective-permute-start.19 = (f32[256,256]{1,0:T(8,128)S(1)}, f32[256,256]{1,0:T(8,128)S(1)}, u32[]{:S(2)}, u32[]{:S(2)}) collective-permute-start(f32[256,256]{1,0:T(8,128)S(1)} %get-tuple-element.132), channel_id=1, source_target_pairs={{0,2},{6,4},{1,3},{4,6},{5,7},{8,10},{14,12},{9,11},{12,14},{13,15... | collective-permute-start | bytes 786440 | tf_op jit(solution)/shard_map/ppermute | solution.py:64
  77.6 5.7 %collective-permute-start.21 = (f32[256,256]{1,0:T(8,128)S(1)}, f32[256,256]{1,0:T(8,128)S(1)}, u32[]{:S(2)}, u32[]{:S(2)}) collective-permute-start(f32[256,256]{1,0:T(8,128)S(1)} %get-tuple-element.136), channel_id=1, source_target_pairs={{0,2},{6,4},{1,3},{7,5},{4,6},{2,0},{5,7},{8,10},{14,12},{9,11},{1... | collective-permute-start | bytes 786440 | tf_op jit(solution)/shard_map/ppermute | solution.py:64
  84.1 1.8 fusion.36
  86.9 1.9 collective-permute-done.21
  89.6 9.6 %collective-permute-start.25 = (f32[256,256]{1,0:T(8,128)S(1)}, f32[256,256]{1,0:T(8,128)S(1)}, u32[]{:S(2)}, u32[]{:S(2)}) collective-permute-start(f32[256,256]{1,0:T(8,128)S(1)} %add_select_fusion.22), channel_id=1, source_target_pairs={{6,4},{0,2},{7,5},{4,6},{2,0},{5,7},{14,12},{8,10},{15,13},{12,14}... | collective-permute-start | bytes 786440 | tf_op jit(solution)/shard_map/ppermute | solution.py:64
  99.9 1.9 fusion.63
  104.3 9.7 %collective-permute-start.30 = (f32[256,256]{1,0:T(8,128)S(1)}, f32[256,256]{1,0:T(8,128)S(1)}, u32[]{:S(2)}, u32[]{:S(2)}) collective-permute-start(f32[256,256]{1,0:T(8,128)S(1)} %get-tuple-element.152), channel_id=1, source_target_pairs={{6,4},{0,2},{7,5},{4,6},{2,0},{5,7},{14,12},{8,10},{15,13},{12,14}... | collective-permute-start | bytes 786440 | tf_op jit(solution)/shard_map/ppermute | solution.py:64
  114.7 1.8 fusion.39
  119.2 8.3 %collective-permute-start.34 = (f32[256,256]{1,0:T(8,128)S(1)}, f32[256,256]{1,0:T(8,128)S(1)}, u32[]{:S(2)}, u32[]{:S(2)}) collective-permute-start(f32[256,256]{1,0:T(8,128)S(1)} %add_select_fusion.18), channel_id=1, source_target_pairs={{6,4},{0,2},{7,5},{2,0},{4,6},{3,1},{5,7},{14,12},{8,10},{15,13},{... | collective-permute-start | bytes 786440 | tf_op jit(solution)/shard_map/ppermute | solution.py:64
  128.2 1.9 fusion.66
  132.3 1.4 collective-permute-done.34
  134.5 7.2 %collective-permute-start.39 = (f32[256,256]{1,0:T(8,128)S(1)}, f32[256,256]{1,0:T(8,128)S(1)}, u32[]{:S(2)}, u32[]{:S(2)}) collective-permute-start(f32[256,256]{1,0:T(8,128)S(1)} %get-tuple-element.168), channel_id=1, source_target_pairs={{6,4},{0,2},{7,5},{2,0},{4,6},{3,1},{5,7},{14,12},{8,10},{15,13},{... | collective-permute-start | bytes 786440 | tf_op jit(solution)/shard_map/ppermute | solution.py:64
  142.6 1.8 fusion.42
  146.9 8.9 %collective-permute-start.43 = (f32[256,256]{1,0:T(8,128)S(1)}, f32[256,256]{1,0:T(8,128)S(1)}, u32[]{:S(2)}, u32[]{:S(2)}) collective-permute-start(f32[256,256]{1,0:T(8,128)S(1)} %add_select_fusion.14), channel_id=1, source_target_pairs={{6,4},{0,2},{7,5},{2,0},{4,6},{3,1},{5,7},{14,12},{8,10},{15,13},{... | collective-permute-start | bytes 786440 | tf_op jit(solution)/shard_map/ppermute | solution.py:64
  156.7 1.6 collective-permute-start.45
  158.2 2.8 %collective-permute-done.43 = f32[256,256]{1,0:T(8,128)S(1)} collective-permute-done((f32[256,256]{1,0:T(8,128)S(1)}, f32[256,256]{1,0:T(8,128)S(1)}, u32[]{:S(2)}, u32[]{:S(2)}) %collective-permute-start.43) | collective-permute-done | bytes 262176 | tf_op jit(solution)/shard_map/ppermute | solution.py:64
  161.8 7.9 %collective-permute-start.47 = (f32[256,256]{1,0:T(8,128)S(1)}, f32[256,256]{1,0:T(8,128)S(1)}, u32[]{:S(2)}, u32[]{:S(2)}) collective-permute-start(f32[256,256]{1,0:T(8,128)S(1)} %get-tuple-element.184), channel_id=1, source_target_pairs={{6,4},{0,2},{7,5},{2,0},{4,6},{3,1},{5,7},{14,12},{8,10},{15,13},{... | collective-permute-start | bytes 786440 | tf_op jit(solution)/shard_map/ppermute | solution.py:64
  172.0 3.7 %collective-permute-done.47 = f32[256,256]{1,0:T(8,128)S(1)} collective-permute-done((f32[256,256]{1,0:T(8,128)S(1)}, f32[256,256]{1,0:T(8,128)S(1)}, u32[]{:S(2)}, u32[]{:S(2)}) %collective-permute-start.47) | collective-permute-done | bytes 262176 | tf_op jit(solution)/shard_map/ppermute | solution.py:64
  179.3 3.7 %collective-permute-done.49 = f32[256,256]{1,0:T(8,128)S(1)} collective-permute-done((f32[256,256]{1,0:T(8,128)S(1)}, f32[256,256]{1,0:T(8,128)S(1)}, u32[]{:S(2)}, u32[]{:S(2)}) %collective-permute-start.49) | collective-permute-done | bytes 262176 | tf_op jit(solution)/shard_map/ppermute | solution.py:64
  184.3 4.0 %collective-permute-done.51 = f32[256,256]{1,0:T(8,128)S(1)} collective-permute-done((f32[256,256]{1,0:T(8,128)S(1)}, f32[256,256]{1,0:T(8,128)S(1)}, u32[]{:S(2)}, u32[]{:S(2)}) %collective-permute-start.51) | collective-permute-done | bytes 262176 | tf_op jit(solution)/shard_map/ppermute | solution.py:64
  188.4 1.5 collective-permute-start.53
  190.0 6.9 %collective-permute-done.54 = f32[256,256]{1,0:T(8,128)S(1)} collective-permute-done((f32[256,256]{1,0:T(8,128)S(1)}, f32[256,256]{1,0:T(8,128)S(1)}, u32[]{:S(2)}, u32[]{:S(2)}) %collective-permute-start.54) | collective-permute-done | bytes 262176 | tf_op jit(solution)/shard_map/ppermute | solution.py:64
  197.1 2.7 %collective-permute-done.53 = f32[256,256]{1,0:T(8,128)S(1)} collective-permute-done((f32[256,256]{1,0:T(8,128)S(1)}, f32[256,256]{1,0:T(8,128)S(1)}, u32[]{:S(2)}, u32[]{:S(2)}) %collective-permute-start.53) | collective-permute-done | bytes 262176 | tf_op jit(solution)/shard_map/ppermute | solution.py:64
  202.4 1.9 collective-permute-done.55
  204.4 1.6 collective-permute-start.56
  205.9 1.5 collective-permute-start.58
  207.4 5.3 %collective-permute-done.56 = f32[256,256]{1,0:T(8,128)S(1)} collective-permute-done((f32[256,256]{1,0:T(8,128)S(1)}, f32[256,256]{1,0:T(8,128)S(1)}, u32[]{:S(2)}, u32[]{:S(2)}) %collective-permute-start.56) | collective-permute-done | bytes 262176 | tf_op jit(solution)/shard_map/ppermute | solution.py:294
  214.1 1.6 collective-permute-start.57
  216.2 5.2 %collective-permute-done.57 = f32[256,256]{1,0:T(8,128)S(1)} collective-permute-done((f32[256,256]{1,0:T(8,128)S(1)}, f32[256,256]{1,0:T(8,128)S(1)}, u32[]{:S(2)}, u32[]{:S(2)}) %collective-permute-start.57) | collective-permute-done | bytes 262176 | tf_op jit(solution)/shard_map/ppermute | solution.py:296
  225.2 5.5 %collective-permute-done.61 = f32[256,128]{1,0:T(8,128)S(1)} collective-permute-done((f32[256,128]{1,0:T(8,128)S(1)}, f32[256,128]{1,0:T(8,128)S(1)}, u32[]{:S(2)}, u32[]{:S(2)}) %collective-permute-start.61) | collective-permute-done | bytes 131104 | tf_op jit(solution)/shard_map/ppermute | solution.py:317
  232.2 7.0 %collective-permute-done.62 = f32[256,128]{1,0:T(8,128)S(1)} collective-permute-done((f32[256,128]{1,0:T(8,128)S(1)}, f32[256,128]{1,0:T(8,128)S(1)}, u32[]{:S(2)}, u32[]{:S(2)}) %collective-permute-start.62) | collective-permute-done | bytes 131104 | tf_op jit(solution)/shard_map/ppermute | solution.py:317
  240.7 10.8 %whiten.1 = f32[1024,256]{1,0:T(8,128)} custom-call(f32[256,256]{1,0:T(8,128)S(1)} %pad_maximum_fusion.2.gram_ref, f32[1024,256]{1,0:T(8,128)S(1)} %pad_maximum_fusion.merged_ref), custom_call_target="tpu_custom_call" | custom-call | tf_op jit(solution)/shard_map/whiten/pallas_call | solution.py:182
  (186 shorter events, 49.7 us)
Async XLA Ops:
  5.2 11.6 %collective-permute-start = (f32[256,256]{1,0:T(8,128)S(1)}, f32[256,256]{1,0:T(8,128)}, u32[]{:S(2)}, u32[]{:S(2)}) collective-permute-start(f32[256,256]{1,0:T(8,128)S(1)} %get-tuple-element.249), channel_id=1, source_target_pairs={{0,2},{6,4},{1,3},{8,10},{14,12},{9,11},{16,18},{22,20},{17,19},{2... | collective-permute-start | bytes 786440 | tf_op jit(solution)/shard_map/ppermute | solution.py:64
  10.8 13.6 %collective-permute-start.1 = (f32[256,256]{1,0:T(8,128)}, f32[256,256]{1,0:T(8,128)S(1)}, u32[]{:S(2)}, u32[]{:S(2)}) collective-permute-start(f32[256,256]{1,0:T(8,128)} %get-tuple-element.250), channel_id=1, source_target_pairs={{0,2},{6,4},{1,3},{7,5},{8,10},{14,12},{9,11},{15,13},{16,18},{22,... | collective-permute-start | bytes 786440 | tf_op jit(solution)/shard_map/ppermute | solution.py:64
  17.8 11.1 %collective-permute-start.2 = (f32[256,256]{1,0:T(8,128)S(1)}, f32[256,256]{1,0:T(8,128)}, u32[]{:S(2)}, u32[]{:S(2)}) collective-permute-start(f32[256,256]{1,0:T(8,128)S(1)} %get-tuple-element.102), channel_id=1, source_target_pairs={{0,2},{6,4},{1,3},{8,10},{14,12},{9,11},{16,18},{22,20},{17,19},{2... | collective-permute-start | bytes 786440 | tf_op jit(solution)/shard_map/ppermute | solution.py:64
  24.5 10.5 %collective-permute-start.4 = (f32[256,256]{1,0:T(8,128)S(1)}, f32[256,256]{1,0:T(8,128)S(1)}, u32[]{:S(2)}, u32[]{:S(2)}) collective-permute-start(f32[256,256]{1,0:T(8,128)S(1)} %get-tuple-element.104), channel_id=1, source_target_pairs={{0,2},{6,4},{1,3},{7,5},{8,10},{14,12},{9,11},{15,13},{16,18},{22,... | collective-permute-start | bytes 786440 | tf_op jit(solution)/shard_map/ppermute | solution.py:64
  27.0 8.0 %collective-permute-start.5 = (f32[256,256]{1,0:T(8,128)S(1)}, f32[256,256]{1,0:T(8,128)S(1)}, u32[]{:S(2)}, u32[]{:S(2)}) collective-permute-start(f32[256,256]{1,0:T(8,128)S(1)} %slice_add_fusion.23), channel_id=1, source_target_pairs={{2,4},{4,2},{3,5},{10,12},{12,10},{11,13},{18,20},{20,18},{19,21},... | collective-permute-start | bytes 786440 | tf_op jit(solution)/shard_map/ppermute | solution.py:66
  30.3 12.6 %collective-permute-start.6 = (f32[256,256]{1,0:T(8,128)S(1)}, f32[256,256]{1,0:T(8,128)S(1)}, u32[]{:S(2)}, u32[]{:S(2)}) collective-permute-start(f32[256,256]{1,0:T(8,128)S(1)} %get-tuple-element.108), channel_id=1, source_target_pairs={{0,2},{6,4},{1,3},{4,6},{5,7},{8,10},{14,12},{9,11},{12,14},{13,15... | collective-permute-start | bytes 786440 | tf_op jit(solution)/shard_map/ppermute | solution.py:64
  35.0 8.0 %collective-permute-start.7 = (f32[256,256]{1,0:T(8,128)S(1)}, f32[256,256]{1,0:T(8,128)S(1)}, u32[]{:S(2)}, u32[]{:S(2)}) collective-permute-start(f32[256,256]{1,0:T(8,128)S(1)} %get-tuple-element.113), channel_id=1, source_target_pairs={{2,4},{4,2},{3,5},{10,12},{12,10},{11,13},{18,20},{20,18},{19,21},... | collective-permute-start | bytes 786440 | tf_op jit(solution)/shard_map/ppermute | solution.py:66
  36.7 12.1 %collective-permute-start.8 = (f32[256,256]{1,0:T(8,128)S(1)}, f32[256,256]{1,0:T(8,128)S(1)}, u32[]{:S(2)}, u32[]{:S(2)}) collective-permute-start(f32[256,256]{1,0:T(8,128)S(1)} %add_select_fusion.30), channel_id=1, source_target_pairs={{0,2},{6,4},{1,3},{7,5},{4,6},{2,0},{5,7},{8,10},{14,12},{9,11},{1... | collective-permute-start | bytes 786440 | tf_op jit(solution)/shard_map/ppermute | solution.py:64
  44.1 12.4 %collective-permute-start.10 = (f32[256,256]{1,0:T(8,128)S(1)}, f32[256,256]{1,0:T(8,128)S(1)}, u32[]{:S(2)}, u32[]{:S(2)}) collective-permute-start(f32[256,256]{1,0:T(8,128)S(1)} %get-tuple-element.116), channel_id=1, source_target_pairs={{0,2},{6,4},{1,3},{4,6},{5,7},{8,10},{14,12},{9,11},{12,14},{13,15... | collective-permute-start | bytes 786440 | tf_op jit(solution)/shard_map/ppermute | solution.py:64
  48.9 7.7 %collective-permute-start.11 = (f32[256,256]{1,0:T(8,128)S(1)}, f32[256,256]{1,0:T(8,128)S(1)}, u32[]{:S(2)}, u32[]{:S(2)}) collective-permute-start(f32[256,256]{1,0:T(8,128)S(1)} %get-tuple-element.121), channel_id=1, source_target_pairs={{2,4},{4,2},{3,5},{10,12},{12,10},{11,13},{18,20},{20,18},{19,21},... | collective-permute-start | bytes 786440 | tf_op jit(solution)/shard_map/ppermute | solution.py:66
  49.7 11.8 %collective-permute-start.12 = (f32[256,256]{1,0:T(8,128)S(1)}, f32[256,256]{1,0:T(8,128)S(1)}, u32[]{:S(2)}, u32[]{:S(2)}) collective-permute-start(f32[256,256]{1,0:T(8,128)S(1)} %get-tuple-element.120), channel_id=1, source_target_pairs={{0,2},{6,4},{1,3},{7,5},{4,6},{2,0},{5,7},{8,10},{14,12},{9,11},{1... | collective-permute-start | bytes 786440 | tf_op jit(solution)/shard_map/ppermute | solution.py:64
  56.8 16.1 %collective-permute-start.15 = (f32[256,256]{1,0:T(8,128)S(1)}, f32[256,256]{1,0:T(8,128)S(1)}, u32[]{:S(2)}, u32[]{:S(2)}) collective-permute-start(f32[256,256]{1,0:T(8,128)S(1)} %add_select_fusion.27), channel_id=1, source_target_pairs={{0,2},{6,4},{1,3},{4,6},{5,7},{8,10},{14,12},{9,11},{12,14},{13,15... | collective-permute-start | bytes 786440 | tf_op jit(solution)/shard_map/ppermute | solution.py:64
  61.7 11.2 %collective-permute-start.16 = (f32[256,256]{1,0:T(8,128)S(1)}, f32[256,256]{1,0:T(8,128)S(1)}, u32[]{:S(2)}, u32[]{:S(2)}) collective-permute-start(f32[256,256]{1,0:T(8,128)S(1)} %get-tuple-element.129), channel_id=1, source_target_pairs={{2,4},{4,2},{3,5},{10,12},{12,10},{11,13},{18,20},{20,18},{19,21},... | collective-permute-start | bytes 786440 | tf_op jit(solution)/shard_map/ppermute | solution.py:66
  62.4 14.4 %collective-permute-start.17 = (f32[256,256]{1,0:T(8,128)S(1)}, f32[256,256]{1,0:T(8,128)S(1)}, u32[]{:S(2)}, u32[]{:S(2)}) collective-permute-start(f32[256,256]{1,0:T(8,128)S(1)} %add_select_fusion.26), channel_id=1, source_target_pairs={{0,2},{6,4},{1,3},{7,5},{4,6},{2,0},{5,7},{8,10},{14,12},{9,11},{1... | collective-permute-start | bytes 786440 | tf_op jit(solution)/shard_map/ppermute | solution.py:64
  69.5 7.3 %collective-permute-start.18 = (f32[256,256]{1,0:T(8,128)S(1)}, f32[256,256]{1,0:T(8,128)S(1)}, u32[]{:S(2)}, u32[]{:S(2)}) collective-permute-start(f32[256,256]{1,0:T(8,128)S(1)} %get-tuple-element.133), channel_id=1, source_target_pairs={{2,4},{4,2},{3,5},{10,12},{12,10},{11,13},{18,20},{20,18},{19,21},... | collective-permute-start | bytes 786440 | tf_op jit(solution)/shard_map/ppermute | solution.py:66
  72.2 11.9 %collective-permute-start.14 = (f32[512,256]{0,1:T(8,128)S(1)}, f32[512,256]{0,1:T(8,128)S(1)}, u32[]{:S(2)}, u32[]{:S(2)}) collective-permute-start(f32[512,256]{0,1:T(8,128)S(1)} %fusion.60), channel_id=1, source_target_pairs={{4,5},{5,4},{6,7},{7,6},{12,13},{13,12},{14,15},{15,14},{20,21},{2... | collective-permute-start | bytes 1572872 | tf_op jit(solution)/shard_map/ppermute | solution.py:234
  73.0 13.0 %collective-permute-start.19 = (f32[256,256]{1,0:T(8,128)S(1)}, f32[256,256]{1,0:T(8,128)S(1)}, u32[]{:S(2)}, u32[]{:S(2)}) collective-permute-start(f32[256,256]{1,0:T(8,128)S(1)} %get-tuple-element.132), channel_id=1, source_target_pairs={{0,2},{6,4},{1,3},{4,6},{5,7},{8,10},{14,12},{9,11},{12,14},{13,15... | collective-permute-start | bytes 786440 | tf_op jit(solution)/shard_map/ppermute | solution.py:64
  77.0 9.0 %collective-permute-start.20 = (f32[256,256]{1,0:T(8,128)S(1)}, f32[256,256]{1,0:T(8,128)S(1)}, u32[]{:S(2)}, u32[]{:S(2)}) collective-permute-start(f32[256,256]{1,0:T(8,128)S(1)} %get-tuple-element.137), channel_id=1, source_target_pairs={{2,4},{4,2},{3,5},{10,12},{12,10},{11,13},{18,20},{20,18},{19,21},... | collective-permute-start | bytes 786440 | tf_op jit(solution)/shard_map/ppermute | solution.py:66
  77.6 11.1 %collective-permute-start.21 = (f32[256,256]{1,0:T(8,128)S(1)}, f32[256,256]{1,0:T(8,128)S(1)}, u32[]{:S(2)}, u32[]{:S(2)}) collective-permute-start(f32[256,256]{1,0:T(8,128)S(1)} %get-tuple-element.136), channel_id=1, source_target_pairs={{0,2},{6,4},{1,3},{7,5},{4,6},{2,0},{5,7},{8,10},{14,12},{9,11},{1... | collective-permute-start | bytes 786440 | tf_op jit(solution)/shard_map/ppermute | solution.py:64
  86.2 16.5 %collective-permute-start.23 = (f32[256,256]{1,0:T(8,128)S(1)}, f32[256,256]{1,0:T(8,128)S(1)}, u32[]{:S(2)}, u32[]{:S(2)}) collective-permute-start(f32[256,256]{1,0:T(8,128)S(1)} %add_select_fusion.23), channel_id=1, source_target_pairs={{6,4},{7,5},{4,6},{5,7},{14,12},{15,13},{12,14},{13,15},{22,20},{2... | collective-permute-start | bytes 786440 | tf_op jit(solution)/shard_map/ppermute | solution.py:64
  88.9 13.8 %collective-permute-start.24 = (f32[256,256]{1,0:T(8,128)S(1)}, f32[256,256]{1,0:T(8,128)S(1)}, u32[]{:S(2)}, u32[]{:S(2)}) collective-permute-start(f32[256,256]{1,0:T(8,128)S(1)} %get-tuple-element.145), channel_id=1, source_target_pairs={{2,4},{4,2},{3,5},{10,12},{12,10},{11,13},{18,20},{20,18},{19,21},... | collective-permute-start | bytes 786440 | tf_op jit(solution)/shard_map/ppermute | solution.py:66
  89.6 13.9 %collective-permute-start.25 = (f32[256,256]{1,0:T(8,128)S(1)}, f32[256,256]{1,0:T(8,128)S(1)}, u32[]{:S(2)}, u32[]{:S(2)}) collective-permute-start(f32[256,256]{1,0:T(8,128)S(1)} %add_select_fusion.22), channel_id=1, source_target_pairs={{6,4},{0,2},{7,5},{4,6},{2,0},{5,7},{14,12},{8,10},{15,13},{12,14}... | collective-permute-start | bytes 786440 | tf_op jit(solution)/shard_map/ppermute | solution.py:64
  101.8 12.9 %collective-permute-start.29 = (f32[512,256]{0,1:T(8,128)S(1)}, f32[512,256]{0,1:T(8,128)S(1)}, u32[]{:S(2)}, u32[]{:S(2)}) collective-permute-start(f32[512,256]{0,1:T(8,128)S(1)} %fusion.63), channel_id=1, source_target_pairs={{4,5},{5,4},{6,7},{7,6},{12,13},{13,12},{14,15},{15,14},{20,21},{2... | collective-permute-start | bytes 1572872 | tf_op jit(solution)/shard_map/ppermute | solution.py:234
  102.8 11.9 %collective-permute-start.27 = (f32[256,256]{1,0:T(8,128)S(1)}, f32[256,256]{1,0:T(8,128)S(1)}, u32[]{:S(2)}, u32[]{:S(2)}) collective-permute-start(f32[256,256]{1,0:T(8,128)S(1)} %get-tuple-element.148), channel_id=1, source_target_pairs={{6,4},{7,5},{4,6},{5,7},{14,12},{15,13},{12,14},{13,15},{22,20},{2... | collective-permute-start | bytes 786440 | tf_op jit(solution)/shard_map/ppermute | solution.py:64
  103.5 11.2 %collective-permute-start.28 = (f32[256,256]{1,0:T(8,128)S(1)}, f32[256,256]{1,0:T(8,128)S(1)}, u32[]{:S(2)}, u32[]{:S(2)}) collective-permute-start(f32[256,256]{1,0:T(8,128)S(1)} %get-tuple-element.153), channel_id=1, source_target_pairs={{4,2},{2,4},{5,3},{12,10},{10,12},{13,11},{20,18},{18,20},{21,19},... | collective-permute-start | bytes 786440 | tf_op jit(solution)/shard_map/ppermute | solution.py:66
  104.3 14.0 %collective-permute-start.30 = (f32[256,256]{1,0:T(8,128)S(1)}, f32[256,256]{1,0:T(8,128)S(1)}, u32[]{:S(2)}, u32[]{:S(2)}) collective-permute-start(f32[256,256]{1,0:T(8,128)S(1)} %get-tuple-element.152), channel_id=1, source_target_pairs={{6,4},{0,2},{7,5},{4,6},{2,0},{5,7},{14,12},{8,10},{15,13},{12,14}... | collective-permute-start | bytes 786440 | tf_op jit(solution)/shard_map/ppermute | solution.py:64
  116.8 14.0 %collective-permute-start.32 = (f32[256,256]{1,0:T(8,128)S(1)}, f32[256,256]{1,0:T(8,128)S(1)}, u32[]{:S(2)}, u32[]{:S(2)}) collective-permute-start(f32[256,256]{1,0:T(8,128)S(1)} %add_select_fusion.19), channel_id=1, source_target_pairs={{6,4},{7,5},{2,0},{4,6},{3,1},{14,12},{15,13},{10,8},{12,14},{11,9... | collective-permute-start | bytes 786440 | tf_op jit(solution)/shard_map/ppermute | solution.py:64
  118.5 12.3 %collective-permute-start.33 = (f32[256,256]{1,0:T(8,128)S(1)}, f32[256,256]{1,0:T(8,128)S(1)}, u32[]{:S(2)}, u32[]{:S(2)}) collective-permute-start(f32[256,256]{1,0:T(8,128)S(1)} %get-tuple-element.161), channel_id=1, source_target_pairs={{4,2},{2,4},{5,3},{12,10},{10,12},{13,11},{20,18},{18,20},{21,19},... | collective-permute-start | bytes 786440 | tf_op jit(solution)/shard_map/ppermute | solution.py:66
  119.2 14.4 %collective-permute-start.34 = (f32[256,256]{1,0:T(8,128)S(1)}, f32[256,256]{1,0:T(8,128)S(1)}, u32[]{:S(2)}, u32[]{:S(2)}) collective-permute-start(f32[256,256]{1,0:T(8,128)S(1)} %add_select_fusion.18), channel_id=1, source_target_pairs={{6,4},{0,2},{7,5},{2,0},{4,6},{3,1},{5,7},{14,12},{8,10},{15,13},{... | collective-permute-start | bytes 786440 | tf_op jit(solution)/shard_map/ppermute | solution.py:64
  130.1 12.5 %collective-permute-start.38 = (f32[512,256]{0,1:T(8,128)S(1)}, f32[512,256]{0,1:T(8,128)S(1)}, u32[]{:S(2)}, u32[]{:S(2)}) collective-permute-start(f32[512,256]{0,1:T(8,128)S(1)} %fusion.66), channel_id=1, source_target_pairs={{4,5},{5,4},{6,7},{7,6},{12,13},{13,12},{14,15},{15,14},{20,21},{2... | collective-permute-start | bytes 1572872 | tf_op jit(solution)/shard_map/ppermute | solution.py:234
  131.0 11.4 %collective-permute-start.36 = (f32[256,256]{1,0:T(8,128)S(1)}, f32[256,256]{1,0:T(8,128)S(1)}, u32[]{:S(2)}, u32[]{:S(2)}) collective-permute-start(f32[256,256]{1,0:T(8,128)S(1)} %get-tuple-element.164), channel_id=1, source_target_pairs={{6,4},{7,5},{2,0},{4,6},{3,1},{14,12},{15,13},{10,8},{12,14},{11,9... | collective-permute-start | bytes 786440 | tf_op jit(solution)/shard_map/ppermute | solution.py:64
  133.7 8.7 %collective-permute-start.37 = (f32[256,256]{1,0:T(8,128)S(1)}, f32[256,256]{1,0:T(8,128)S(1)}, u32[]{:S(2)}, u32[]{:S(2)}) collective-permute-start(f32[256,256]{1,0:T(8,128)S(1)} %get-tuple-element.169), channel_id=1, source_target_pairs={{4,2},{2,4},{5,3},{12,10},{10,12},{13,11},{20,18},{18,20},{21,19},... | collective-permute-start | bytes 786440 | tf_op jit(solution)/shard_map/ppermute | solution.py:66
  134.5 11.6 %collective-permute-start.39 = (f32[256,256]{1,0:T(8,128)S(1)}, f32[256,256]{1,0:T(8,128)S(1)}, u32[]{:S(2)}, u32[]{:S(2)}) collective-permute-start(f32[256,256]{1,0:T(8,128)S(1)} %get-tuple-element.168), channel_id=1, source_target_pairs={{6,4},{0,2},{7,5},{2,0},{4,6},{3,1},{5,7},{14,12},{8,10},{15,13},{... | collective-permute-start | bytes 786440 | tf_op jit(solution)/shard_map/ppermute | solution.py:64
  144.5 12.0 %collective-permute-start.41 = (f32[256,256]{1,0:T(8,128)S(1)}, f32[256,256]{1,0:T(8,128)S(1)}, u32[]{:S(2)}, u32[]{:S(2)}) collective-permute-start(f32[256,256]{1,0:T(8,128)S(1)} %add_select_fusion.15), channel_id=1, source_target_pairs={{6,4},{7,5},{2,0},{4,6},{3,1},{14,12},{15,13},{10,8},{12,14},{11,9... | collective-permute-start | bytes 786440 | tf_op jit(solution)/shard_map/ppermute | solution.py:64
  146.0 10.5 %collective-permute-start.42 = (f32[256,256]{1,0:T(8,128)S(1)}, f32[256,256]{1,0:T(8,128)S(1)}, u32[]{:S(2)}, u32[]{:S(2)}) collective-permute-start(f32[256,256]{1,0:T(8,128)S(1)} %get-tuple-element.177), channel_id=1, source_target_pairs={{4,2},{2,4},{5,3},{12,10},{10,12},{13,11},{20,18},{18,20},{21,19},... | collective-permute-start | bytes 786440 | tf_op jit(solution)/shard_map/ppermute | solution.py:66
  146.9 14.1 %collective-permute-start.43 = (f32[256,256]{1,0:T(8,128)S(1)}, f32[256,256]{1,0:T(8,128)S(1)}, u32[]{:S(2)}, u32[]{:S(2)}) collective-permute-start(f32[256,256]{1,0:T(8,128)S(1)} %add_select_fusion.14), channel_id=1, source_target_pairs={{6,4},{0,2},{7,5},{2,0},{4,6},{3,1},{5,7},{14,12},{8,10},{15,13},{... | collective-permute-start | bytes 786440 | tf_op jit(solution)/shard_map/ppermute | solution.py:64
  156.7 13.8 %collective-permute-start.45 = (f32[256,256]{1,0:T(8,128)S(1)}, f32[256,256]{1,0:T(8,128)S(1)}, u32[]{:S(2)}, u32[]{:S(2)}) collective-permute-start(f32[256,256]{1,0:T(8,128)S(1)} %get-tuple-element.180), channel_id=1, source_target_pairs={{6,4},{7,5},{2,0},{4,6},{3,1},{14,12},{15,13},{10,8},{12,14},{11,9... | collective-permute-start | bytes 786440 | tf_op jit(solution)/shard_map/ppermute | solution.py:64
  161.0 9.4 %collective-permute-start.46 = (f32[256,256]{1,0:T(8,128)S(1)}, f32[256,256]{1,0:T(8,128)S(1)}, u32[]{:S(2)}, u32[]{:S(2)}) collective-permute-start(f32[256,256]{1,0:T(8,128)S(1)} %get-tuple-element.185), channel_id=1, source_target_pairs={{4,2},{2,4},{5,3},{12,10},{10,12},{13,11},{20,18},{18,20},{21,19},... | collective-permute-start | bytes 786440 | tf_op jit(solution)/shard_map/ppermute | solution.py:66
  161.8 13.9 %collective-permute-start.47 = (f32[256,256]{1,0:T(8,128)S(1)}, f32[256,256]{1,0:T(8,128)S(1)}, u32[]{:S(2)}, u32[]{:S(2)}) collective-permute-start(f32[256,256]{1,0:T(8,128)S(1)} %get-tuple-element.184), channel_id=1, source_target_pairs={{6,4},{0,2},{7,5},{2,0},{4,6},{3,1},{5,7},{14,12},{8,10},{15,13},{... | collective-permute-start | bytes 786440 | tf_op jit(solution)/shard_map/ppermute | solution.py:64
  170.7 12.3 %collective-permute-start.49 = (f32[256,256]{1,0:T(8,128)S(1)}, f32[256,256]{1,0:T(8,128)S(1)}, u32[]{:S(2)}, u32[]{:S(2)}) collective-permute-start(f32[256,256]{1,0:T(8,128)S(1)} %add.304), channel_id=1, source_target_pairs={{2,0},{4,6},{3,1},{10,8},{12,14},{11,9},{18,16},{20,22},{19,17},{2... | collective-permute-start | bytes 786440 | tf_op jit(solution)/shard_map/ppermute | solution.py:64
  176.5 11.8 %collective-permute-start.51 = (f32[256,256]{1,0:T(8,128)S(1)}, f32[256,256]{1,0:T(8,128)S(1)}, u32[]{:S(2)}, u32[]{:S(2)}) collective-permute-start(f32[256,256]{1,0:T(8,128)S(1)} %add.308), channel_id=1, source_target_pairs={{2,0},{4,6},{3,1},{5,7},{10,8},{12,14},{11,9},{13,15},{18,16},{20,... | collective-permute-start | bytes 786440 | tf_op jit(solution)/shard_map/ppermute | solution.py:64
  177.8 10.5 %collective-permute-start.52 = (f32[256,256]{1,0:T(8,128)S(1)}, f32[256,256]{1,0:T(8,128)S(1)}, u32[]{:S(2)}, u32[]{:S(2)}) collective-permute-start(f32[256,256]{1,0:T(8,128)S(1)} %get-tuple-element.195), channel_id=1, source_target_pairs={{4,2},{2,4},{5,3},{12,10},{10,12},{13,11},{20,18},{18,20},{21,19},... | collective-permute-start | bytes 786440 | tf_op jit(solution)/shard_map/ppermute | solution.py:66
  183.0 13.9 %collective-permute-start.54 = (f32[256,256]{1,0:T(8,128)S(1)}, f32[256,256]{1,0:T(8,128)S(1)}, u32[]{:S(2)}, u32[]{:S(2)}) collective-permute-start(f32[256,256]{1,0:T(8,128)S(1)} %add.310), channel_id=1, source_target_pairs={{2,0},{4,6},{3,1},{10,8},{12,14},{11,9},{18,16},{20,22},{19,17},{2... | collective-permute-start | bytes 786440 | tf_op jit(solution)/shard_map/ppermute | solution.py:64
  188.4 11.4 %collective-permute-start.53 = (f32[256,256]{1,0:T(8,128)S(1)}, f32[256,256]{1,0:T(8,128)S(1)}, u32[]{:S(2)}, u32[]{:S(2)}) collective-permute-start(f32[256,256]{1,0:T(8,128)S(1)} %add.311), channel_id=1, source_target_pairs={{2,0},{4,6},{3,1},{5,7},{10,8},{12,14},{11,9},{13,15},{18,16},{20,... | collective-permute-start | bytes 786440 | tf_op jit(solution)/shard_map/ppermute | solution.py:64
  204.4 8.4 %collective-permute-start.56 = (f32[256,256]{1,0:T(8,128)S(1)}, f32[256,256]{1,0:T(8,128)S(1)}, u32[]{:S(2)}, u32[]{:S(2)}) collective-permute-start(f32[256,256]{1,0:T(8,128)S(1)} %get-tuple-element.265), channel_id=1, source_target_pairs={{0,8},{8,0},{16,24},{24,16},{1,9},{9,1},{17,25},{25,17},{2,10},{10... | collective-permute-start | bytes 786440 | tf_op jit(solution)/shard_map/ppermute | solution.py:294
  205.9 8.1 %collective-permute-start.58 = (f32[256,256]{1,0:T(8,128)S(1)}, f32[256,256]{1,0:T(8,128)S(1)}, u32[]{:S(2)}, u32[]{:S(2)}) collective-permute-start(f32[256,256]{1,0:T(8,128)S(1)} %get-tuple-element.266), channel_id=1, source_target_pairs={{0,16},{8,24},{16,0},{24,8},{1,17},{9,25},{17,1},{25,9},{2,18},{10... | collective-permute-start | bytes 786440 | tf_op jit(solution)/shard_map/ppermute | solution.py:295
  223.8 15.5 %collective-permute-start.64 = (f32[512,256]{1,0:T(8,128)S(1)}, f32[512,256]{1,0:T(8,128)S(1)}, u32[]{:S(2)}, u32[]{:S(2)}) collective-permute-start(f32[512,256]{1,0:T(8,128)S(1)} %pad_maximum_fusion.1), channel_id=1, source_target_pairs={{0,1},{1,0},{2,3},{3,2},{4,5},{5,4},{6,7},{7,6},{8,9},{9,8},{10,11... | collective-permute-start | bytes 1572872 | tf_op jit(solution)/shard_map/ppermute | solution.py:299
  230.7 8.5 %collective-permute-start.62 = (f32[256,128]{1,0:T(8,128)S(1)}, f32[256,128]{1,0:T(8,128)S(1)}, u32[]{:S(2)}, u32[]{:S(2)}) collective-permute-start(f32[256,128]{1,0:T(8,128)S(1)} %add.324), channel_id=1, source_target_pairs={{0,4},{2,6},{4,0},{6,2},{1,5},{3,7},{5,1},{7,3},{8,12},{10,14},{12... | collective-permute-start | bytes 393224 | tf_op jit(solution)/shard_map/ppermute | solution.py:317
  (27 other events, 254.8 us)

commit v2 on v1

--- a/solution.py
+++ b/solution.py
@@ -256,20 +256,24 @@
 
     if use_line:
         line = Line(LANES, sent_index, col_index)
-        for term, first in zip(terms, firsts):
-            line.step(term, first, True)
-        done = 0
-        while done < len(slots):
-            while done + per_view - 1 not in line.finals:
-                line.step()
-            proj = [line.finals[done + q] * keep_of(*slots[done + q]) for q in range(per_view)]
-            for q, term in enumerate(back_terms(proj, slots[done][0])):
-                line.step(term, firsts[q], False)
-            done += per_view
-        begin = line.slot - len(slots)
+        count, cut_at = len(slots), len(slots) - per_view // 2
+        plan = [(True, k) for k in range(cut_at)]
+        for k in range(count):
+            if k < count - cut_at:
+                plan += [(True, cut_at + k)]
+            plan += [(False, k)]
+        backs, begun = [], {}
+        for spread, k in plan:
+            if not spread and k == len(backs):
+                while any(begun[k + q] not in line.finals for q in range(per_view)):
+                    line.step()
+                proj = [line.finals[begun[k + q]] * keep_of(*slots[k + q]) for q in range(per_view)]
+                backs += back_terms(proj, slots[k][0])
+            begun[k if spread else count + k] = line.slot
+            line.step(terms[k] if spread else backs[k], firsts[k], spread)
         for _ in range(3 * LANES):
             line.step()
-        sums = [line.finals[begin + k] for k in range(len(slots))]
+        sums = [line.finals[begun[count + k]] for k in range(count)]
     else:
         sums = []
         for j in range(view_count):

time: 253 us -> 261 us (1.032)
  waiting for transfers between devices: 58.4 us -> 62.7 us
  starting transfers between devices: 146 us -> 149 us
    ppermute x28, waiting for transfers between devices: 29.2 us -> 33.4 us  [step(): ends_in = lax.ppermute(ends, axes, perm)]
    ppermute x28, starting transfers between devices: 121 us -> 124 us  [step(): ends_in = lax.ppermute(ends, axes, perm)]
  transfers between devices with their start and end apart: 65 -> 65, of which waited for: 21 -> 20; matrix products, arithmetic and copies ran while one was open for 10% -> 10% of each run, Pallas kernels for 0% -> 0%
where the time goes in v2:
time: 261 us; the launch traced here: 259 us
  starting transfers between devices  149 us (57%)
  waiting for transfers between devices  62.7 us (24%)
  matrix products  22.2 us (9%)
  Pallas kernels  10.8 us (4%)
  other arithmetic  8.36 us (3%)
  local copies, waits for them, and re-layouts  4.42 us (2%)
    ppermute x28, starting transfers between devices, step(): ends_in = lax.ppermute(ends, axes, perm)  124 us
    ppermute x28, waiting for transfers between devices, step(): ends_in = lax.ppermute(ends, axes, perm)  33.4 us
    ppermute x24, starting transfers between devices, step(): pair_in = lax.ppermute(pair, axes, self.pairs_of(middle, 1))  16.9 us
    ppermute x2, waiting for transfers between devices, shards(): lax.ppermute(gram, 'sent', [(s, s ^ bit) for s in range(sent_size)])  12.5 us
    pallas_call x1, Pallas kernels, whiten(): pl.pallas_call(functools.partial(whiten_kernel, scale), out_shape=jax.Sha...  10.8 us
    dot_general x3, matrix products, term_of(): lax.dot_general(features, shared, down, preferred_element_type=jnp.float32)  7.79 us
    dot_general x3, matrix products, first_half(): half_part = jnp.dot(inv_factor[j], proj, precision=high)  5.78 us
    dot_general x3, matrix products, back_terms(): lax.dot_general(inv_factor[j], first_half(proj, j), down, precision=high,...  5.5 us
  transfers between devices with their start and end apart: 65, of which 20 were waited for; matrix products, arithmetic and copies ran while one was open for 10% of the time, Pallas kernels for 0%

profile of v2, /device:TPU:0, one launch (start us, length us, event | category | flops | bytes accessed | tf_op | source)
XLA Modules:
  0.0 259.3 jit_solution(6087405091693963238)
XLA Ops:
  1.7 2.8 %fusion.45 = f32[1024,256]{1,0:T(8,128)S(1)} fusion(bf16[1024,256]{1,0:T(8,128)(2,1)S(1)} %copy-done, bf16[3,1024,1024]{2,1,0:T(8,128)(2,1)} %param.4), kind=kOutput, calls=%fused_computation.39 | convolution fusion | flops 537133056 | bytes 3670016 | tf_op jit(solution)/shard_map/dot_general | solution.py:243
  5.2 5.7 %collective-permute-start = (f32[256,256]{1,0:T(8,128)S(1)}, f32[256,256]{1,0:T(8,128)}, u32[]{:S(2)}, u32[]{:S(2)}) collective-permute-start(f32[256,256]{1,0:T(8,128)S(1)} %get-tuple-element.248), channel_id=1, source_target_pairs={{0,2},{6,4},{1,3},{8,10},{14,12},{9,11},{16,18},{22,20},{17,19},{2... | collective-permute-start | bytes 786440 | tf_op jit(solution)/shard_map/ppermute | solution.py:64
  10.9 2.0 collective-permute-start.1
  12.9 1.7 fusion.54
  14.6 3.3 %fusion.57 = f32[1024,256]{1,0:T(8,128)} fusion(bf16[1024,256]{1,0:T(8,128)(2,1)S(1)} %copy-done, bf16[3,1024,1024]{2,1,0:T(8,128)(2,1)} %param.4), kind=kOutput, calls=%fused_computation.43 | convolution fusion | flops 537133056 | bytes 3670016 | tf_op jit(solution)/shard_map/dot_general | solution.py:243
  18.1 2.0 fusion.175
  20.1 3.9 %collective-permute-start.2 = (f32[256,256]{1,0:T(8,128)}, f32[256,256]{1,0:T(8,128)}, u32[]{:S(2)}, u32[]{:S(2)}) collective-permute-start(f32[256,256]{1,0:T(8,128)} %get-tuple-element.102), channel_id=1, source_target_pairs={{0,2},{6,4},{1,3},{8,10},{14,12},{9,11},{16,18},{22,20},{17,19},{2... | collective-permute-start | bytes 786440 | tf_op jit(solution)/shard_map/ppermute | solution.py:64
  26.5 2.3 collective-permute-start.4
  30.7 4.4 %collective-permute-start.6 = (f32[256,256]{1,0:T(8,128)S(1)}, f32[256,256]{1,0:T(8,128)S(1)}, u32[]{:S(2)}, u32[]{:S(2)}) collective-permute-start(f32[256,256]{1,0:T(8,128)S(1)} %get-tuple-element.108), channel_id=1, source_target_pairs={{0,2},{6,4},{1,3},{4,6},{5,7},{8,10},{14,12},{9,11},{12,14},{13,15... | collective-permute-start | bytes 786440 | tf_op jit(solution)/shard_map/ppermute | solution.py:64
  36.7 5.5 %collective-permute-start.8 = (f32[256,256]{1,0:T(8,128)S(1)}, f32[256,256]{1,0:T(8,128)S(1)}, u32[]{:S(2)}, u32[]{:S(2)}) collective-permute-start(f32[256,256]{1,0:T(8,128)S(1)} %add_select_fusion.30), channel_id=1, source_target_pairs={{0,2},{6,4},{1,3},{7,5},{4,6},{2,0},{5,7},{8,10},{14,12},{9,11},{1... | collective-permute-start | bytes 786440 | tf_op jit(solution)/shard_map/ppermute | solution.py:64
  43.0 5.8 %collective-permute-start.10 = (f32[256,256]{1,0:T(8,128)S(1)}, f32[256,256]{1,0:T(8,128)S(1)}, u32[]{:S(2)}, u32[]{:S(2)}) collective-permute-start(f32[256,256]{1,0:T(8,128)S(1)} %get-tuple-element.116), channel_id=1, source_target_pairs={{0,2},{6,4},{1,3},{4,6},{5,7},{8,10},{14,12},{9,11},{12,14},{13,15... | collective-permute-start | bytes 786440 | tf_op jit(solution)/shard_map/ppermute | solution.py:64
  49.6 6.8 %collective-permute-start.12 = (f32[256,256]{1,0:T(8,128)S(1)}, f32[256,256]{1,0:T(8,128)S(1)}, u32[]{:S(2)}, u32[]{:S(2)}) collective-permute-start(f32[256,256]{1,0:T(8,128)S(1)} %get-tuple-element.120), channel_id=1, source_target_pairs={{0,2},{6,4},{1,3},{7,5},{4,6},{2,0},{5,7},{8,10},{14,12},{9,11},{1... | collective-permute-start | bytes 786440 | tf_op jit(solution)/shard_map/ppermute | solution.py:64
  57.4 4.4 %collective-permute-start.15 = (f32[256,256]{1,0:T(8,128)S(1)}, f32[256,256]{1,0:T(8,128)S(1)}, u32[]{:S(2)}, u32[]{:S(2)}) collective-permute-start(f32[256,256]{1,0:T(8,128)S(1)} %add_select_fusion.27), channel_id=1, source_target_pairs={{0,2},{6,4},{1,3},{4,6},{5,7},{8,10},{14,12},{9,11},{12,14},{13,15... | collective-permute-start | bytes 786440 | tf_op jit(solution)/shard_map/ppermute | solution.py:64
  62.6 1.9 fusion.60
  65.3 6.5 %collective-permute-start.17 = (f32[256,256]{1,0:T(8,128)S(1)}, f32[256,256]{1,0:T(8,128)S(1)}, u32[]{:S(2)}, u32[]{:S(2)}) collective-permute-start(f32[256,256]{1,0:T(8,128)S(1)} %add_select_fusion.26), channel_id=1, source_target_pairs={{0,2},{6,4},{1,3},{7,5},{4,6},{2,0},{5,7},{8,10},{14,12},{9,11},{1... | collective-permute-start | bytes 786440 | tf_op jit(solution)/shard_map/ppermute | solution.py:64
  72.7 5.9 %collective-permute-start.19 = (f32[256,256]{1,0:T(8,128)S(1)}, f32[256,256]{1,0:T(8,128)S(1)}, u32[]{:S(2)}, u32[]{:S(2)}) collective-permute-start(f32[256,256]{1,0:T(8,128)S(1)} %get-tuple-element.132), channel_id=1, source_target_pairs={{0,2},{6,4},{1,3},{4,6},{5,7},{8,10},{14,12},{9,11},{12,14},{13,15... | collective-permute-start | bytes 786440 | tf_op jit(solution)/shard_map/ppermute | solution.py:64
  79.4 1.8 fusion.36
  84.6 10.4 %collective-permute-start.23 = (f32[256,256]{1,0:T(8,128)S(1)}, f32[256,256]{1,0:T(8,128)S(1)}, u32[]{:S(2)}, u32[]{:S(2)}) collective-permute-start(f32[256,256]{1,0:T(8,128)S(1)} %get-tuple-element.140), channel_id=1, source_target_pairs={{0,2},{6,4},{1,3},{7,5},{4,6},{5,7},{8,10},{14,12},{9,11},{15,13},... | collective-permute-start | bytes 786440 | tf_op jit(solution)/shard_map/ppermute | solution.py:64
  96.1 5.4 %collective-permute-start.25 = (f32[256,256]{1,0:T(8,128)S(1)}, f32[256,256]{1,0:T(8,128)S(1)}, u32[]{:S(2)}, u32[]{:S(2)}) collective-permute-start(f32[256,256]{1,0:T(8,128)S(1)} %get-tuple-element.144), channel_id=1, source_target_pairs={{6,4},{0,2},{7,5},{4,6},{2,0},{5,7},{14,12},{8,10},{15,13},{12,14}... | collective-permute-start | bytes 786440 | tf_op jit(solution)/shard_map/ppermute | solution.py:64
  102.2 1.9 fusion.63
  106.7 9.0 %collective-permute-start.30 = (f32[256,256]{1,0:T(8,128)S(1)}, f32[256,256]{1,0:T(8,128)S(1)}, u32[]{:S(2)}, u32[]{:S(2)}) collective-permute-start(f32[256,256]{1,0:T(8,128)S(1)} %get-tuple-element.152), channel_id=1, source_target_pairs={{6,4},{0,2},{7,5},{2,0},{4,6},{3,1},{14,12},{8,10},{15,13},{10,8},... | collective-permute-start | bytes 786440 | tf_op jit(solution)/shard_map/ppermute | solution.py:64
  116.6 1.8 fusion.39
  119.8 1.9 collective-permute-done.30
  122.5 7.7 %collective-permute-start.34 = (f32[256,256]{1,0:T(8,128)S(1)}, f32[256,256]{1,0:T(8,128)S(1)}, u32[]{:S(2)}, u32[]{:S(2)}) collective-permute-start(f32[256,256]{1,0:T(8,128)S(1)} %add_select_fusion.18), channel_id=1, source_target_pairs={{6,4},{0,2},{7,5},{2,0},{4,6},{3,1},{5,7},{14,12},{8,10},{15,13},{... | collective-permute-start | bytes 786440 | tf_op jit(solution)/shard_map/ppermute | solution.py:64
  132.3 2.9 %collective-permute-done.34 = f32[256,256]{1,0:T(8,128)S(1)} collective-permute-done((f32[256,256]{1,0:T(8,128)S(1)}, f32[256,256]{1,0:T(8,128)S(1)}, u32[]{:S(2)}, u32[]{:S(2)}) %collective-permute-start.34) | collective-permute-done | bytes 262176 | tf_op jit(solution)/shard_map/ppermute | solution.py:64
  135.9 1.9 fusion.66
  138.6 8.9 %collective-permute-start.39 = (f32[256,256]{1,0:T(8,128)S(1)}, f32[256,256]{1,0:T(8,128)S(1)}, u32[]{:S(2)}, u32[]{:S(2)}) collective-permute-start(f32[256,256]{1,0:T(8,128)S(1)} %get-tuple-element.168), channel_id=1, source_target_pairs={{6,4},{0,2},{7,5},{2,0},{4,6},{3,1},{5,7},{14,12},{8,10},{15,13},{... | collective-permute-start | bytes 786440 | tf_op jit(solution)/shard_map/ppermute | solution.py:64
  148.4 1.8 fusion.42
  151.6 2.8 %collective-permute-done.39 = f32[256,256]{1,0:T(8,128)S(1)} collective-permute-done((f32[256,256]{1,0:T(8,128)S(1)}, f32[256,256]{1,0:T(8,128)S(1)}, u32[]{:S(2)}, u32[]{:S(2)}) %collective-permute-start.39) | collective-permute-done | bytes 262176 | tf_op jit(solution)/shard_map/ppermute | solution.py:64
  155.3 7.4 %collective-permute-start.43 = (f32[256,256]{1,0:T(8,128)S(1)}, f32[256,256]{1,0:T(8,128)S(1)}, u32[]{:S(2)}, u32[]{:S(2)}) collective-permute-start(f32[256,256]{1,0:T(8,128)S(1)} %add_select_fusion.14), channel_id=1, source_target_pairs={{6,4},{0,2},{7,5},{2,0},{4,6},{3,1},{5,7},{14,12},{8,10},{15,13},{... | collective-permute-start | bytes 786440 | tf_op jit(solution)/shard_map/ppermute | solution.py:64
  163.5 1.4 collective-permute-start.45
  164.9 2.0 collective-permute-done.43
  167.8 8.8 %collective-permute-start.47 = (f32[256,256]{1,0:T(8,128)S(1)}, f32[256,256]{1,0:T(8,128)S(1)}, u32[]{:S(2)}, u32[]{:S(2)}) collective-permute-start(f32[256,256]{1,0:T(8,128)S(1)} %get-tuple-element.184), channel_id=1, source_target_pairs={{6,4},{0,2},{7,5},{2,0},{4,6},{3,1},{5,7},{14,12},{8,10},{15,13},{... | collective-permute-start | bytes 786440 | tf_op jit(solution)/shard_map/ppermute | solution.py:64
  178.8 2.7 %collective-permute-done.47 = f32[256,256]{1,0:T(8,128)S(1)} collective-permute-done((f32[256,256]{1,0:T(8,128)S(1)}, f32[256,256]{1,0:T(8,128)S(1)}, u32[]{:S(2)}, u32[]{:S(2)}) %collective-permute-start.47) | collective-permute-done | bytes 262176 | tf_op jit(solution)/shard_map/ppermute | solution.py:64
  185.1 5.0 %collective-permute-done.49 = f32[256,256]{1,0:T(8,128)S(1)} collective-permute-done((f32[256,256]{1,0:T(8,128)S(1)}, f32[256,256]{1,0:T(8,128)S(1)}, u32[]{:S(2)}, u32[]{:S(2)}) %collective-permute-start.49) | collective-permute-done | bytes 262176 | tf_op jit(solution)/shard_map/ppermute | solution.py:64
  191.4 4.0 %collective-permute-done.51 = f32[256,256]{1,0:T(8,128)S(1)} collective-permute-done((f32[256,256]{1,0:T(8,128)S(1)}, f32[256,256]{1,0:T(8,128)S(1)}, u32[]{:S(2)}, u32[]{:S(2)}) %collective-permute-start.51) | collective-permute-done | bytes 262176 | tf_op jit(solution)/shard_map/ppermute | solution.py:64
  195.5 1.5 collective-permute-start.53
  197.1 7.6 %collective-permute-done.54 = f32[256,256]{1,0:T(8,128)S(1)} collective-permute-done((f32[256,256]{1,0:T(8,128)S(1)}, f32[256,256]{1,0:T(8,128)S(1)}, u32[]{:S(2)}, u32[]{:S(2)}) %collective-permute-start.54) | collective-permute-done | bytes 262176 | tf_op jit(solution)/shard_map/ppermute | solution.py:64
  204.9 2.6 %collective-permute-done.53 = f32[256,256]{1,0:T(8,128)S(1)} collective-permute-done((f32[256,256]{1,0:T(8,128)S(1)}, f32[256,256]{1,0:T(8,128)S(1)}, u32[]{:S(2)}, u32[]{:S(2)}) %collective-permute-start.53) | collective-permute-done | bytes 262176 | tf_op jit(solution)/shard_map/ppermute | solution.py:64
  210.2 1.9 collective-permute-done.55
  212.2 1.5 collective-permute-start.56
  213.7 1.5 collective-permute-start.58
  215.2 5.3 %collective-permute-done.56 = f32[256,256]{1,0:T(8,128)S(1)} collective-permute-done((f32[256,256]{1,0:T(8,128)S(1)}, f32[256,256]{1,0:T(8,128)S(1)}, u32[]{:S(2)}, u32[]{:S(2)}) %collective-permute-start.56) | collective-permute-done | bytes 262176 | tf_op jit(solution)/shard_map/ppermute | solution.py:298
  221.9 1.6 collective-permute-start.57
  224.0 5.1 %collective-permute-done.57 = f32[256,256]{1,0:T(8,128)S(1)} collective-permute-done((f32[256,256]{1,0:T(8,128)S(1)}, f32[256,256]{1,0:T(8,128)S(1)}, u32[]{:S(2)}, u32[]{:S(2)}) %collective-permute-start.57) | collective-permute-done | bytes 262176 | tf_op jit(solution)/shard_map/ppermute | solution.py:300
  233.0 5.5 %collective-permute-done.61 = f32[256,128]{1,0:T(8,128)S(1)} collective-permute-done((f32[256,128]{1,0:T(8,128)S(1)}, f32[256,128]{1,0:T(8,128)S(1)}, u32[]{:S(2)}, u32[]{:S(2)}) %collective-permute-start.61) | collective-permute-done | bytes 131104 | tf_op jit(solution)/shard_map/ppermute | solution.py:321
  240.0 7.0 %collective-permute-done.62 = f32[256,128]{1,0:T(8,128)S(1)} collective-permute-done((f32[256,128]{1,0:T(8,128)S(1)}, f32[256,128]{1,0:T(8,128)S(1)}, u32[]{:S(2)}, u32[]{:S(2)}) %collective-permute-start.62) | collective-permute-done | bytes 131104 | tf_op jit(solution)/shard_map/ppermute | solution.py:321
  248.5 10.8 %whiten.1 = f32[1024,256]{1,0:T(8,128)} custom-call(f32[256,256]{1,0:T(8,128)S(1)} %pad_maximum_fusion.2.gram_ref, f32[1024,256]{1,0:T(8,128)S(1)} %pad_maximum_fusion.merged_ref), custom_call_target="tpu_custom_call" | custom-call | tf_op jit(solution)/shard_map/whiten/pallas_call | solution.py:182
  (189 shorter events, 50.7 us)
Async XLA Ops:
  5.2 12.9 %collective-permute-start = (f32[256,256]{1,0:T(8,128)S(1)}, f32[256,256]{1,0:T(8,128)}, u32[]{:S(2)}, u32[]{:S(2)}) collective-permute-start(f32[256,256]{1,0:T(8,128)S(1)} %get-tuple-element.248), channel_id=1, source_target_pairs={{0,2},{6,4},{1,3},{8,10},{14,12},{9,11},{16,18},{22,20},{17,19},{2... | collective-permute-start | bytes 786440 | tf_op jit(solution)/shard_map/ppermute | solution.py:64
  10.9 14.5 %collective-permute-start.1 = (f32[256,256]{1,0:T(8,128)}, f32[256,256]{1,0:T(8,128)}, u32[]{:S(2)}, u32[]{:S(2)}) collective-permute-start(f32[256,256]{1,0:T(8,128)} %get-tuple-element.249), channel_id=1, source_target_pairs={{0,2},{6,4},{1,3},{7,5},{8,10},{14,12},{9,11},{15,13},{16,18},{22,... | collective-permute-start | bytes 786440 | tf_op jit(solution)/shard_map/ppermute | solution.py:64
  20.1 9.5 %collective-permute-start.2 = (f32[256,256]{1,0:T(8,128)}, f32[256,256]{1,0:T(8,128)}, u32[]{:S(2)}, u32[]{:S(2)}) collective-permute-start(f32[256,256]{1,0:T(8,128)} %get-tuple-element.102), channel_id=1, source_target_pairs={{0,2},{6,4},{1,3},{8,10},{14,12},{9,11},{16,18},{22,20},{17,19},{2... | collective-permute-start | bytes 786440 | tf_op jit(solution)/shard_map/ppermute | solution.py:64
  26.5 9.4 %collective-permute-start.4 = (f32[256,256]{1,0:T(8,128)}, f32[256,256]{1,0:T(8,128)S(1)}, u32[]{:S(2)}, u32[]{:S(2)}) collective-permute-start(f32[256,256]{1,0:T(8,128)} %get-tuple-element.104), channel_id=1, source_target_pairs={{0,2},{6,4},{1,3},{7,5},{8,10},{14,12},{9,11},{15,13},{16,18},{22,... | collective-permute-start | bytes 786440 | tf_op jit(solution)/shard_map/ppermute | solution.py:64
  28.8 7.0 %collective-permute-start.5 = (f32[256,256]{1,0:T(8,128)S(1)}, f32[256,256]{1,0:T(8,128)S(1)}, u32[]{:S(2)}, u32[]{:S(2)}) collective-permute-start(f32[256,256]{1,0:T(8,128)S(1)} %slice_add_fusion.23), channel_id=1, source_target_pairs={{2,4},{4,2},{3,5},{10,12},{12,10},{11,13},{18,20},{20,18},{19,21},... | collective-permute-start | bytes 786440 | tf_op jit(solution)/shard_map/ppermute | solution.py:66
  30.7 12.2 %collective-permute-start.6 = (f32[256,256]{1,0:T(8,128)S(1)}, f32[256,256]{1,0:T(8,128)S(1)}, u32[]{:S(2)}, u32[]{:S(2)}) collective-permute-start(f32[256,256]{1,0:T(8,128)S(1)} %get-tuple-element.108), channel_id=1, source_target_pairs={{0,2},{6,4},{1,3},{4,6},{5,7},{8,10},{14,12},{9,11},{12,14},{13,15... | collective-permute-start | bytes 786440 | tf_op jit(solution)/shard_map/ppermute | solution.py:64
  36.7 12.1 %collective-permute-start.8 = (f32[256,256]{1,0:T(8,128)S(1)}, f32[256,256]{1,0:T(8,128)S(1)}, u32[]{:S(2)}, u32[]{:S(2)}) collective-permute-start(f32[256,256]{1,0:T(8,128)S(1)} %add_select_fusion.30), channel_id=1, source_target_pairs={{0,2},{6,4},{1,3},{7,5},{4,6},{2,0},{5,7},{8,10},{14,12},{9,11},{1... | collective-permute-start | bytes 786440 | tf_op jit(solution)/shard_map/ppermute | solution.py:64
  43.0 14.1 %collective-permute-start.10 = (f32[256,256]{1,0:T(8,128)S(1)}, f32[256,256]{1,0:T(8,128)S(1)}, u32[]{:S(2)}, u32[]{:S(2)}) collective-permute-start(f32[256,256]{1,0:T(8,128)S(1)} %get-tuple-element.116), channel_id=1, source_target_pairs={{0,2},{6,4},{1,3},{4,6},{5,7},{8,10},{14,12},{9,11},{12,14},{13,15... | collective-permute-start | bytes 786440 | tf_op jit(solution)/shard_map/ppermute | solution.py:64
  48.8 8.3 %collective-permute-start.11 = (f32[256,256]{1,0:T(8,128)S(1)}, f32[256,256]{1,0:T(8,128)S(1)}, u32[]{:S(2)}, u32[]{:S(2)}) collective-permute-start(f32[256,256]{1,0:T(8,128)S(1)} %get-tuple-element.121), channel_id=1, source_target_pairs={{2,4},{4,2},{3,5},{10,12},{12,10},{11,13},{18,20},{20,18},{19,21},... | collective-permute-start | bytes 786440 | tf_op jit(solution)/shard_map/ppermute | solution.py:66
  49.6 12.2 %collective-permute-start.12 = (f32[256,256]{1,0:T(8,128)S(1)}, f32[256,256]{1,0:T(8,128)S(1)}, u32[]{:S(2)}, u32[]{:S(2)}) collective-permute-start(f32[256,256]{1,0:T(8,128)S(1)} %get-tuple-element.120), channel_id=1, source_target_pairs={{0,2},{6,4},{1,3},{7,5},{4,6},{2,0},{5,7},{8,10},{14,12},{9,11},{1... | collective-permute-start | bytes 786440 | tf_op jit(solution)/shard_map/ppermute | solution.py:64
  57.4 15.1 %collective-permute-start.15 = (f32[256,256]{1,0:T(8,128)S(1)}, f32[256,256]{1,0:T(8,128)S(1)}, u32[]{:S(2)}, u32[]{:S(2)}) collective-permute-start(f32[256,256]{1,0:T(8,128)S(1)} %add_select_fusion.27), channel_id=1, source_target_pairs={{0,2},{6,4},{1,3},{4,6},{5,7},{8,10},{14,12},{9,11},{12,14},{13,15... | collective-permute-start | bytes 786440 | tf_op jit(solution)/shard_map/ppermute | solution.py:64
  61.8 10.8 %collective-permute-start.16 = (f32[256,256]{1,0:T(8,128)S(1)}, f32[256,256]{1,0:T(8,128)S(1)}, u32[]{:S(2)}, u32[]{:S(2)}) collective-permute-start(f32[256,256]{1,0:T(8,128)S(1)} %get-tuple-element.129), channel_id=1, source_target_pairs={{2,4},{4,2},{3,5},{10,12},{12,10},{11,13},{18,20},{20,18},{19,21},... | collective-permute-start | bytes 786440 | tf_op jit(solution)/shard_map/ppermute | solution.py:66
  64.6 14.9 %collective-permute-start.14 = (f32[512,256]{0,1:T(8,128)S(1)}, f32[512,256]{0,1:T(8,128)S(1)}, u32[]{:S(2)}, u32[]{:S(2)}) collective-permute-start(f32[512,256]{0,1:T(8,128)S(1)} %fusion.60), channel_id=1, source_target_pairs={{4,5},{5,4},{6,7},{7,6},{12,13},{13,12},{14,15},{15,14},{20,21},{2... | collective-permute-start | bytes 1572872 | tf_op jit(solution)/shard_map/ppermute | solution.py:234
  65.3 13.3 %collective-permute-start.17 = (f32[256,256]{1,0:T(8,128)S(1)}, f32[256,256]{1,0:T(8,128)S(1)}, u32[]{:S(2)}, u32[]{:S(2)}) collective-permute-start(f32[256,256]{1,0:T(8,128)S(1)} %add_select_fusion.26), channel_id=1, source_target_pairs={{0,2},{6,4},{1,3},{7,5},{4,6},{2,0},{5,7},{8,10},{14,12},{9,11},{1... | collective-permute-start | bytes 786440 | tf_op jit(solution)/shard_map/ppermute | solution.py:64
  72.7 11.9 %collective-permute-start.19 = (f32[256,256]{1,0:T(8,128)S(1)}, f32[256,256]{1,0:T(8,128)S(1)}, u32[]{:S(2)}, u32[]{:S(2)}) collective-permute-start(f32[256,256]{1,0:T(8,128)S(1)} %get-tuple-element.132), channel_id=1, source_target_pairs={{0,2},{6,4},{1,3},{4,6},{5,7},{8,10},{14,12},{9,11},{12,14},{13,15... | collective-permute-start | bytes 786440 | tf_op jit(solution)/shard_map/ppermute | solution.py:64
  81.3 14.6 %collective-permute-start.21 = (f32[256,256]{1,0:T(8,128)S(1)}, f32[256,256]{1,0:T(8,128)S(1)}, u32[]{:S(2)}, u32[]{:S(2)}) collective-permute-start(f32[256,256]{1,0:T(8,128)S(1)} %add_select_fusion.24), channel_id=1, source_target_pairs={{6,4},{7,5},{4,6},{2,0},{5,7},{14,12},{15,13},{12,14},{10,8},{13,1... | collective-permute-start | bytes 786440 | tf_op jit(solution)/shard_map/ppermute | solution.py:64
  82.6 13.3 %collective-permute-start.22 = (f32[256,256]{1,0:T(8,128)S(1)}, f32[256,256]{1,0:T(8,128)S(1)}, u32[]{:S(2)}, u32[]{:S(2)}) collective-permute-start(f32[256,256]{1,0:T(8,128)S(1)} %get-tuple-element.141), channel_id=1, source_target_pairs={{2,4},{4,2},{3,5},{10,12},{12,10},{11,13},{18,20},{20,18},{19,21},... | collective-permute-start | bytes 786440 | tf_op jit(solution)/shard_map/ppermute | solution.py:66
  84.6 20.4 %collective-permute-start.23 = (f32[256,256]{1,0:T(8,128)S(1)}, f32[256,256]{1,0:T(8,128)S(1)}, u32[]{:S(2)}, u32[]{:S(2)}) collective-permute-start(f32[256,256]{1,0:T(8,128)S(1)} %get-tuple-element.140), channel_id=1, source_target_pairs={{0,2},{6,4},{1,3},{7,5},{4,6},{5,7},{8,10},{14,12},{9,11},{15,13},... | collective-permute-start | bytes 786440 | tf_op jit(solution)/shard_map/ppermute | solution.py:64
  95.1 10.0 %collective-permute-start.24 = (f32[256,256]{1,0:T(8,128)S(1)}, f32[256,256]{1,0:T(8,128)S(1)}, u32[]{:S(2)}, u32[]{:S(2)}) collective-permute-start(f32[256,256]{1,0:T(8,128)S(1)} %get-tuple-element.145), channel_id=1, source_target_pairs={{2,4},{4,2},{3,5},{10,12},{12,10},{11,13},{18,20},{20,18},{19,21},... | collective-permute-start | bytes 786440 | tf_op jit(solution)/shard_map/ppermute | solution.py:66
  96.1 10.5 %collective-permute-start.25 = (f32[256,256]{1,0:T(8,128)S(1)}, f32[256,256]{1,0:T(8,128)S(1)}, u32[]{:S(2)}, u32[]{:S(2)}) collective-permute-start(f32[256,256]{1,0:T(8,128)S(1)} %get-tuple-element.144), channel_id=1, source_target_pairs={{6,4},{0,2},{7,5},{4,6},{2,0},{5,7},{14,12},{8,10},{15,13},{12,14}... | collective-permute-start | bytes 786440 | tf_op jit(solution)/shard_map/ppermute | solution.py:64
  104.1 12.5 %collective-permute-start.29 = (f32[512,256]{0,1:T(8,128)S(1)}, f32[512,256]{0,1:T(8,128)S(1)}, u32[]{:S(2)}, u32[]{:S(2)}) collective-permute-start(f32[512,256]{0,1:T(8,128)S(1)} %fusion.63), channel_id=1, source_target_pairs={{4,5},{5,4},{6,7},{7,6},{12,13},{13,12},{14,15},{15,14},{20,21},{2... | collective-permute-start | bytes 1572872 | tf_op jit(solution)/shard_map/ppermute | solution.py:234
  105.2 11.3 %collective-permute-start.27 = (f32[256,256]{1,0:T(8,128)S(1)}, f32[256,256]{1,0:T(8,128)S(1)}, u32[]{:S(2)}, u32[]{:S(2)}) collective-permute-start(f32[256,256]{1,0:T(8,128)S(1)} %add_select_fusion.21), channel_id=1, source_target_pairs={{6,4},{7,5},{4,6},{5,7},{14,12},{15,13},{12,14},{13,15},{22,20},{2... | collective-permute-start | bytes 786440 | tf_op jit(solution)/shard_map/ppermute | solution.py:64
  105.9 10.6 %collective-permute-start.28 = (f32[256,256]{1,0:T(8,128)S(1)}, f32[256,256]{1,0:T(8,128)S(1)}, u32[]{:S(2)}, u32[]{:S(2)}) collective-permute-start(f32[256,256]{1,0:T(8,128)S(1)} %get-tuple-element.153), channel_id=1, source_target_pairs={{2,4},{4,2},{3,5},{10,12},{12,10},{11,13},{18,20},{20,18},{19,21},... | collective-permute-start | bytes 786440 | tf_op jit(solution)/shard_map/ppermute | solution.py:66
  106.7 14.9 %collective-permute-start.30 = (f32[256,256]{1,0:T(8,128)S(1)}, f32[256,256]{1,0:T(8,128)S(1)}, u32[]{:S(2)}, u32[]{:S(2)}) collective-permute-start(f32[256,256]{1,0:T(8,128)S(1)} %get-tuple-element.152), channel_id=1, source_target_pairs={{6,4},{0,2},{7,5},{2,0},{4,6},{3,1},{14,12},{8,10},{15,13},{10,8},... | collective-permute-start | bytes 786440 | tf_op jit(solution)/shard_map/ppermute | solution.py:64
  118.5 12.4 %collective-permute-start.32 = (f32[256,256]{1,0:T(8,128)S(1)}, f32[256,256]{1,0:T(8,128)S(1)}, u32[]{:S(2)}, u32[]{:S(2)}) collective-permute-start(f32[256,256]{1,0:T(8,128)S(1)} %add_select_fusion.19), channel_id=1, source_target_pairs={{6,4},{7,5},{4,6},{2,0},{5,7},{14,12},{15,13},{12,14},{10,8},{13,1... | collective-permute-start | bytes 786440 | tf_op jit(solution)/shard_map/ppermute | solution.py:64
  121.7 9.2 %collective-permute-start.33 = (f32[256,256]{1,0:T(8,128)S(1)}, f32[256,256]{1,0:T(8,128)S(1)}, u32[]{:S(2)}, u32[]{:S(2)}) collective-permute-start(f32[256,256]{1,0:T(8,128)S(1)} %get-tuple-element.161), channel_id=1, source_target_pairs={{4,2},{2,4},{5,3},{12,10},{10,12},{13,11},{20,18},{18,20},{21,19},... | collective-permute-start | bytes 786440 | tf_op jit(solution)/shard_map/ppermute | solution.py:66
  122.5 12.7 %collective-permute-start.34 = (f32[256,256]{1,0:T(8,128)S(1)}, f32[256,256]{1,0:T(8,128)S(1)}, u32[]{:S(2)}, u32[]{:S(2)}) collective-permute-start(f32[256,256]{1,0:T(8,128)S(1)} %add_select_fusion.18), channel_id=1, source_target_pairs={{6,4},{0,2},{7,5},{2,0},{4,6},{3,1},{5,7},{14,12},{8,10},{15,13},{... | collective-permute-start | bytes 786440 | tf_op jit(solution)/shard_map/ppermute | solution.py:64
  131.0 17.2 %collective-permute-start.36 = (f32[256,256]{1,0:T(8,128)S(1)}, f32[256,256]{1,0:T(8,128)S(1)}, u32[]{:S(2)}, u32[]{:S(2)}) collective-permute-start(f32[256,256]{1,0:T(8,128)S(1)} %get-tuple-element.164), channel_id=1, source_target_pairs={{6,4},{7,5},{2,0},{4,6},{3,1},{14,12},{15,13},{10,8},{12,14},{11,9... | collective-permute-start | bytes 786440 | tf_op jit(solution)/shard_map/ppermute | solution.py:64
  135.2 13.1 %collective-permute-start.37 = (f32[256,256]{1,0:T(8,128)S(1)}, f32[256,256]{1,0:T(8,128)S(1)}, u32[]{:S(2)}, u32[]{:S(2)}) collective-permute-start(f32[256,256]{1,0:T(8,128)S(1)} %get-tuple-element.169), channel_id=1, source_target_pairs={{4,2},{2,4},{5,3},{12,10},{10,12},{13,11},{20,18},{18,20},{21,19},... | collective-permute-start | bytes 786440 | tf_op jit(solution)/shard_map/ppermute | solution.py:66
  137.8 10.6 %collective-permute-start.38 = (f32[512,256]{0,1:T(8,128)S(1)}, f32[512,256]{0,1:T(8,128)S(1)}, u32[]{:S(2)}, u32[]{:S(2)}) collective-permute-start(f32[512,256]{0,1:T(8,128)S(1)} %fusion.66), channel_id=1, source_target_pairs={{4,5},{5,4},{6,7},{7,6},{12,13},{13,12},{14,15},{15,14},{20,21},{2... | collective-permute-start | bytes 1572872 | tf_op jit(solution)/shard_map/ppermute | solution.py:234
  138.6 15.8 %collective-permute-start.39 = (f32[256,256]{1,0:T(8,128)S(1)}, f32[256,256]{1,0:T(8,128)S(1)}, u32[]{:S(2)}, u32[]{:S(2)}) collective-permute-start(f32[256,256]{1,0:T(8,128)S(1)} %get-tuple-element.168), channel_id=1, source_target_pairs={{6,4},{0,2},{7,5},{2,0},{4,6},{3,1},{5,7},{14,12},{8,10},{15,13},{... | collective-permute-start | bytes 786440 | tf_op jit(solution)/shard_map/ppermute | solution.py:64
  150.3 13.1 %collective-permute-start.41 = (f32[256,256]{1,0:T(8,128)S(1)}, f32[256,256]{1,0:T(8,128)S(1)}, u32[]{:S(2)}, u32[]{:S(2)}) collective-permute-start(f32[256,256]{1,0:T(8,128)S(1)} %add_select_fusion.15), channel_id=1, source_target_pairs={{6,4},{7,5},{2,0},{4,6},{3,1},{14,12},{15,13},{10,8},{12,14},{11,9... | collective-permute-start | bytes 786440 | tf_op jit(solution)/shard_map/ppermute | solution.py:64
  154.4 9.0 %collective-permute-start.42 = (f32[256,256]{1,0:T(8,128)S(1)}, f32[256,256]{1,0:T(8,128)S(1)}, u32[]{:S(2)}, u32[]{:S(2)}) collective-permute-start(f32[256,256]{1,0:T(8,128)S(1)} %get-tuple-element.177), channel_id=1, source_target_pairs={{4,2},{2,4},{5,3},{12,10},{10,12},{13,11},{20,18},{18,20},{21,19},... | collective-permute-start | bytes 786440 | tf_op jit(solution)/shard_map/ppermute | solution.py:66
  155.3 11.7 %collective-permute-start.43 = (f32[256,256]{1,0:T(8,128)S(1)}, f32[256,256]{1,0:T(8,128)S(1)}, u32[]{:S(2)}, u32[]{:S(2)}) collective-permute-start(f32[256,256]{1,0:T(8,128)S(1)} %add_select_fusion.14), channel_id=1, source_target_pairs={{6,4},{0,2},{7,5},{2,0},{4,6},{3,1},{5,7},{14,12},{8,10},{15,13},{... | collective-permute-start | bytes 786440 | tf_op jit(solution)/shard_map/ppermute | solution.py:64
  163.5 13.7 %collective-permute-start.45 = (f32[256,256]{1,0:T(8,128)S(1)}, f32[256,256]{1,0:T(8,128)S(1)}, u32[]{:S(2)}, u32[]{:S(2)}) collective-permute-start(f32[256,256]{1,0:T(8,128)S(1)} %get-tuple-element.180), channel_id=1, source_target_pairs={{6,4},{7,5},{2,0},{4,6},{3,1},{14,12},{15,13},{10,8},{12,14},{11,9... | collective-permute-start | bytes 786440 | tf_op jit(solution)/shard_map/ppermute | solution.py:64
  167.0 10.3 %collective-permute-start.46 = (f32[256,256]{1,0:T(8,128)S(1)}, f32[256,256]{1,0:T(8,128)S(1)}, u32[]{:S(2)}, u32[]{:S(2)}) collective-permute-start(f32[256,256]{1,0:T(8,128)S(1)} %get-tuple-element.185), channel_id=1, source_target_pairs={{4,2},{2,4},{5,3},{12,10},{10,12},{13,11},{20,18},{18,20},{21,19},... | collective-permute-start | bytes 786440 | tf_op jit(solution)/shard_map/ppermute | solution.py:66
  167.8 13.7 %collective-permute-start.47 = (f32[256,256]{1,0:T(8,128)S(1)}, f32[256,256]{1,0:T(8,128)S(1)}, u32[]{:S(2)}, u32[]{:S(2)}) collective-permute-start(f32[256,256]{1,0:T(8,128)S(1)} %get-tuple-element.184), channel_id=1, source_target_pairs={{6,4},{0,2},{7,5},{2,0},{4,6},{3,1},{5,7},{14,12},{8,10},{15,13},{... | collective-permute-start | bytes 786440 | tf_op jit(solution)/shard_map/ppermute | solution.py:64
  177.5 12.6 %collective-permute-start.49 = (f32[256,256]{1,0:T(8,128)S(1)}, f32[256,256]{1,0:T(8,128)S(1)}, u32[]{:S(2)}, u32[]{:S(2)}) collective-permute-start(f32[256,256]{1,0:T(8,128)S(1)} %add.304), channel_id=1, source_target_pairs={{2,0},{4,6},{3,1},{10,8},{12,14},{11,9},{18,16},{20,22},{19,17},{2... | collective-permute-start | bytes 786440 | tf_op jit(solution)/shard_map/ppermute | solution.py:64
  181.7 8.4 %collective-permute-start.50 = (f32[256,256]{1,0:T(8,128)S(1)}, f32[256,256]{1,0:T(8,128)S(1)}, u32[]{:S(2)}, u32[]{:S(2)}) collective-permute-start(f32[256,256]{1,0:T(8,128)S(1)} %get-tuple-element.193), channel_id=1, source_target_pairs={{4,2},{2,4},{5,3},{12,10},{10,12},{13,11},{20,18},{18,20},{21,19},... | collective-permute-start | bytes 786440 | tf_op jit(solution)/shard_map/ppermute | solution.py:66
  182.3 13.1 %collective-permute-start.51 = (f32[256,256]{1,0:T(8,128)S(1)}, f32[256,256]{1,0:T(8,128)S(1)}, u32[]{:S(2)}, u32[]{:S(2)}) collective-permute-start(f32[256,256]{1,0:T(8,128)S(1)} %add.308), channel_id=1, source_target_pairs={{2,0},{4,6},{3,1},{5,7},{10,8},{12,14},{11,9},{13,15},{18,16},{20,... | collective-permute-start | bytes 786440 | tf_op jit(solution)/shard_map/ppermute | solution.py:64
  183.6 11.8 %collective-permute-start.52 = (f32[256,256]{1,0:T(8,128)S(1)}, f32[256,256]{1,0:T(8,128)S(1)}, u32[]{:S(2)}, u32[]{:S(2)}) collective-permute-start(f32[256,256]{1,0:T(8,128)S(1)} %get-tuple-element.195), channel_id=1, source_target_pairs={{4,2},{2,4},{5,3},{12,10},{10,12},{13,11},{20,18},{18,20},{21,19},... | collective-permute-start | bytes 786440 | tf_op jit(solution)/shard_map/ppermute | solution.py:66
  190.1 14.6 %collective-permute-start.54 = (f32[256,256]{1,0:T(8,128)S(1)}, f32[256,256]{1,0:T(8,128)S(1)}, u32[]{:S(2)}, u32[]{:S(2)}) collective-permute-start(f32[256,256]{1,0:T(8,128)S(1)} %add.310), channel_id=1, source_target_pairs={{2,0},{4,6},{3,1},{10,8},{12,14},{11,9},{18,16},{20,22},{19,17},{2... | collective-permute-start | bytes 786440 | tf_op jit(solution)/shard_map/ppermute | solution.py:64
  195.5 12.0 %collective-permute-start.53 = (f32[256,256]{1,0:T(8,128)S(1)}, f32[256,256]{1,0:T(8,128)S(1)}, u32[]{:S(2)}, u32[]{:S(2)}) collective-permute-start(f32[256,256]{1,0:T(8,128)S(1)} %add.311), channel_id=1, source_target_pairs={{2,0},{4,6},{3,1},{5,7},{10,8},{12,14},{11,9},{13,15},{18,16},{20,... | collective-permute-start | bytes 786440 | tf_op jit(solution)/shard_map/ppermute | solution.py:64
  212.2 8.4 %collective-permute-start.56 = (f32[256,256]{1,0:T(8,128)S(1)}, f32[256,256]{1,0:T(8,128)S(1)}, u32[]{:S(2)}, u32[]{:S(2)}) collective-permute-start(f32[256,256]{1,0:T(8,128)S(1)} %get-tuple-element.264), channel_id=1, source_target_pairs={{0,8},{8,0},{16,24},{24,16},{1,9},{9,1},{17,25},{25,17},{2,10},{10... | collective-permute-start | bytes 786440 | tf_op jit(solution)/shard_map/ppermute | solution.py:298
  213.7 8.1 %collective-permute-start.58 = (f32[256,256]{1,0:T(8,128)S(1)}, f32[256,256]{1,0:T(8,128)S(1)}, u32[]{:S(2)}, u32[]{:S(2)}) collective-permute-start(f32[256,256]{1,0:T(8,128)S(1)} %get-tuple-element.265), channel_id=1, source_target_pairs={{0,16},{8,24},{16,0},{24,8},{1,17},{9,25},{17,1},{25,9},{2,18},{10... | collective-permute-start | bytes 786440 | tf_op jit(solution)/shard_map/ppermute | solution.py:299
  221.9 7.3 %collective-permute-start.57 = (f32[256,256]{1,0:T(8,128)S(1)}, f32[256,256]{1,0:T(8,128)S(1)}, u32[]{:S(2)}, u32[]{:S(2)}) collective-permute-start(f32[256,256]{1,0:T(8,128)S(1)} %get-tuple-element.262), channel_id=1, source_target_pairs={{0,16},{8,24},{16,0},{24,8},{1,17},{9,25},{17,1},{25,9},{2,18},{10... | collective-permute-start | bytes 786440 | tf_op jit(solution)/shard_map/ppermute | solution.py:300
  231.6 15.5 %collective-permute-start.64 = (f32[512,256]{1,0:T(8,128)S(1)}, f32[512,256]{1,0:T(8,128)S(1)}, u32[]{:S(2)}, u32[]{:S(2)}) collective-permute-start(f32[512,256]{1,0:T(8,128)S(1)} %pad_maximum_fusion.1), channel_id=1, source_target_pairs={{0,1},{1,0},{2,3},{3,2},{4,5},{5,4},{6,7},{7,6},{8,9},{9,8},{10,11... | collective-permute-start | bytes 1572872 | tf_op jit(solution)/shard_map/ppermute | solution.py:303
  238.5 8.5 %collective-permute-start.62 = (f32[256,128]{1,0:T(8,128)S(1)}, f32[256,128]{1,0:T(8,128)S(1)}, u32[]{:S(2)}, u32[]{:S(2)}) collective-permute-start(f32[256,128]{1,0:T(8,128)S(1)} %add.324), channel_id=1, source_target_pairs={{0,4},{2,6},{4,0},{6,2},{1,5},{3,7},{5,1},{7,3},{8,12},{10,14},{12... | collective-permute-start | bytes 393224 | tf_op jit(solution)/shard_map/ppermute | solution.py:321
  (28 other events, 256.9 us)
